TPU v7x, 128 devices: a whole 4x4x4 slice. The times are simulated.
128 devices in a mesh: gx: 16 (over y, x), yz: 8 (over z, core).
Axes of the slice: x: 4, y: 4, z: 4, core: 2. Of those that a mesh axis runs over, the one named last changes fastest.
Arguments:
- positions: float32 [65536, 384], P(('gx', 'yz')), may hold values from 0 to 4
- vectors: float32 [65536, 768], P(('gx', 'yz')), may hold values from -6 to 6
- send_slots: int32 [128, 128, 4], P(('gx', 'yz')), may hold values from -1 to 511, as said below
- pairs: int32 [32768, 2], P(('gx', 'yz')), may hold values from -1 to 511, as said below
- coarse: int32 [65536], P(('gx', 'yz')), may hold values from 0 to 63
Outputs:
- forces: float32 [65536, 384], P(('gx', 'yz'))
Inputs may be any that keep to these rules, and one draw needn't show every extreme that they name: `send_slots`: each (sender, owner) row lists its live slots first and has at most 4 of them; every device sends at least one block to itself; some owner receives 4 blocks from every sender. Each owner's live pairs come first and both entries name live received slots; a -1 row has both entries -1; some owners have 256 live pairs.
All inputs are finite; a program needn't handle non-finite values.
Results may differ from a plain program's by a relative error of at most 0.0003.
Values sent between devices are 32-bit elements; how exact they have to be, the bound alone decides.
A program may use at most 64 MiB of HBM per device.

v0:
```python
import math

import jax
import jax.numpy as jnp
from jax import lax
from jax.sharding import PartitionSpec as P

KC = 64


core_sq = 0.25
far_sq = 1.0


def columns(array, count, width):
    return [array[:, index * width : (index + 1) * width] for index in range(count)]


def inner_sum(left, right):
    return sum((left[index][:, :, None] * right[index][:, None, :] for index in range(3)))


def pair_tile(pos_a, vec_a, pos_b, vec_b, factor, width):
    comp_a = columns(pos_a, 3, width)
    comp_b = columns(pos_b, 3, width)
    offsets = [comp_a[index][:, :, None] - comp_b[index][:, None, :] for index in range(3)]
    distance = offsets[0] ** 2 + offsets[1] ** 2 + offsets[2] ** 2 + core_sq
    parts_a = columns(vec_a, 6, width)
    parts_b = columns(vec_b, 6, width)
    line_a, burg_a = (parts_a[0:3], parts_a[3:6])
    line_b, burg_b = (parts_b[0:3], parts_b[3:6])
    coupling = inner_sum(burg_a, burg_b) * inner_sum(line_a, line_b) + 0.5 * inner_sum(
        burg_a, line_b
    ) * inner_sum(line_a, burg_b)
    weight = coupling * factor / (distance * jnp.sqrt(distance))
    on_a = jnp.concatenate([jnp.sum(weight * offsets[index], axis=2) for index in range(3)], axis=1)
    on_b = jnp.concatenate(
        [-jnp.sum(weight * offsets[index], axis=1) for index in range(3)], axis=1
    )
    return (on_a, on_b)


def far_tile(pos, vec, moments, width):
    cell_ids = jnp.arange(KC)
    centers = (
        jnp.stack([cell_ids // 16, cell_ids // 4 % 4, cell_ids % 4], axis=1).astype(jnp.float32)
        + 0.5
    )
    comps = columns(pos, 3, width)
    offsets = [comps[index][:, None, :] - centers[None, :, index, None] for index in range(3)]
    distance = offsets[0] ** 2 + offsets[1] ** 2 + offsets[2] ** 2 + far_sq
    parts = columns(vec, 6, width)
    line, burg = (parts[0:3], parts[3:6])
    strength = sum(
        (
            burg[k_idx][:, None, :] * moments[None, :, k_idx, l_idx, None] * line[l_idx][:, None, :]
            for k_idx in range(3)
            for l_idx in range(3)
        )
    )
    weight = strength / (math.sqrt(KC) * distance * jnp.sqrt(distance))
    return jnp.concatenate([jnp.sum(weight * offsets[index], axis=1) for index in range(3)], axis=1)


def on_device(positions, vectors, send_slots, pairs, coarse):
    send_ids = send_slots[0]
    devices, capacity = send_ids.shape
    blocks_here = positions.shape[0]
    width = positions.shape[1] // 3
    size_gx = lax.axis_size("gx")
    size_yz = lax.axis_size("yz")
    filled = (send_ids >= 0).astype(jnp.float32)
    slot_ids = jnp.maximum(send_ids, 0)
    out_pos = positions[slot_ids] * filled[:, :, None]
    out_vec = vectors[slot_ids] * filled[:, :, None]
    got_pos, got_vec = (
        lax.all_to_all(out_pos, ("gx", "yz"), split_axis=0, concat_axis=0, tiled=True),
        lax.all_to_all(out_vec, ("gx", "yz"), split_axis=0, concat_axis=0, tiled=True),
    )
    recv_pos = got_pos.reshape(devices * capacity, 3 * width)
    recv_vec = got_vec.reshape(devices * capacity, 6 * width)
    parts = columns(vectors, 6, width)
    line, burg = (parts[0:3], parts[3:6])
    per_block = jnp.stack(
        [jnp.sum(burg[k_idx] * line[l_idx], axis=1) for k_idx in range(3) for l_idx in range(3)],
        axis=1,
    )
    one_hot = (coarse[:, None] == jnp.arange(KC)[None, :]).astype(jnp.float32)
    local_moments = jnp.dot(one_hot.T, per_block, precision=lax.Precision.HIGHEST)
    total_moments = lax.psum(local_moments, ("gx", "yz"))
    all_blocks = blocks_here * size_gx * size_yz
    moments = (total_moments / math.sqrt(all_blocks * width / KC)).reshape(KC, 3, 3)
    pair_count = pairs.shape[0]
    group_size = math.gcd(pair_count, 16)
    usable = (pairs[:, 0] >= 0).astype(jnp.float32)
    pair_ids = jnp.maximum(pairs, 0)
    factor = 1.0 / math.sqrt(width)

    def pair_block(packed):
        ids_group, mask_group = packed
        on_a, on_b = pair_tile(
            recv_pos[ids_group[:, 0]],
            recv_vec[ids_group[:, 0]],
            recv_pos[ids_group[:, 1]],
            recv_vec[ids_group[:, 1]],
            factor,
            width,
        )
        return (on_a * mask_group[:, None], on_b * mask_group[:, None])

    on_a, on_b = lax.map(
        pair_block, (pair_ids.reshape(-1, group_size, 2), usable.reshape(-1, group_size))
    )
    partial_value = jax.ops.segment_sum(
        on_a.reshape(-1, 3 * width), pair_ids[:, 0], num_segments=devices * capacity
    )
    partial_value = partial_value + jax.ops.segment_sum(
        on_b.reshape(-1, 3 * width), pair_ids[:, 1], num_segments=devices * capacity
    )
    returned = lax.all_to_all(
        partial_value.reshape(devices, capacity, 3 * width),
        ("gx", "yz"),
        split_axis=0,
        concat_axis=0,
        tiled=True,
    )
    returned = returned.reshape(devices * capacity, 3 * width) * filled.reshape(-1)[:, None]
    near = jax.ops.segment_sum(returned, slot_ids.reshape(-1), num_segments=blocks_here)
    far_group = math.gcd(blocks_here, 32)
    far = lax.map(
        lambda packed: far_tile(packed[0], packed[1], moments, width),
        (positions.reshape(-1, far_group, 3 * width), vectors.reshape(-1, far_group, 6 * width)),
    )
    return near + far.reshape(blocks_here, 3 * width)


def solution(mesh):
    placed = (
        P(("gx", "yz"), None),
        P(("gx", "yz"), None),
        P(("gx", "yz"), None, None),
        P(("gx", "yz"), None),
        P(("gx", "yz")),
    )
    return jax.shard_map(
        on_device, mesh=mesh, in_specs=placed, out_specs=P(("gx", "yz"), None), check_vma=False
    )
```

profile of v0, /device:TPU:1, one launch (start us, length us, event | category | flops | bytes accessed | tf_op | source)
XLA Modules:
  0.0 422.2 jit_solution(4157428495131071883)
XLA Ops:
  1.7 3.0 gather_fusion.5
  6.0 11.9 %all-to-all-start.1 = ((f32[128,4,384]{2,1,0:T(4,128)}), f32[128,4,384]{2,1,0:T(4,128)}, u32[]{:S(2)}, u32[]{:S(2)}) async-start(f32[128,4,384]{2,1,0:T(4,128)} %broadcast_multiply_fusion.1), calls=%async_computation.1 | async-start | bytes 1572864 | tf_op jit(solution)/shard_map/all_to_all | solution.py:77
  17.9 2.6 gather_fusion.4
  23.8 10.2 %all-to-all-done.1 = f32[128,4,384]{2,1,0:T(4,128)} async-done(((f32[128,4,384]{2,1,0:T(4,128)}), f32[128,4,384]{2,1,0:T(4,128)}, u32[]{:S(2)}, u32[]{:S(2)}) %all-to-all-start.1) | async-done | bytes 786464 | tf_op jit(solution)/shard_map/all_to_all | solution.py:77
  34.0 5.7 %all-to-all-start = ((f32[128,4,768]{2,1,0:T(4,128)}), f32[128,4,768]{2,1,0:T(4,128)}, u32[]{:S(2)}, u32[]{:S(2)}) async-start(f32[128,4,768]{2,1,0:T(4,128)} %broadcast_multiply_fusion), calls=%async_computation | async-start | bytes 3145728 | tf_op jit(solution)/shard_map/all_to_all | solution.py:78
  40.7 74.9 %psum.7 = f32[64,9]{0,1:T(8,128)S(1)} all-reduce(f32[64,9]{0,1:T(8,128)S(1)} %fusion.31), channel_id=1, replica_groups=mesh['gx'=16,'yz'=8] {'gx','yz'}, use_global_device_ids=true, to_apply=%region_9.0 | all-reduce | flops 576 | bytes 4608 | tf_op jit(solution)/shard_map/psum | solution.py:90
  115.9 2.3 reshape.361
  120.0 159.2 %while.26 = (s32[]{:T(128)}, f32[16,16,384]{2,1,0:T(8,128)}, f32[16,16,384]{2,1,0:T(8,128)}, s32[16,16,2]{1,0,2:T(8,128)S(1)}, f32[512,768]{1,0:T(8,128)S(1)}, /...) while((s32[]{:T(128)}, f32[16,16,384]{2,1,0:T(8,128)}, f32[16,16,384]{2,1,0:T(8,128)}, ...), condition=%wide.region_22.23_spmd, body=%wide.region_15.22_spmd.sunk | while | flops 11829346 | bytes 943773 | solution.py:111
  124.7 4.5 %fusion.68 = (f32[16,128]{1,0:T(8,128)S(1)}, f32[16,128]{1,0:T(8,128)S(1)}, f32[16,128]{1,0:T(8,128)S(1)}, f32[16,128]{1,0:T(8,128)S(1)}, f32[16,128]{1,0:T(8,128)S(1)}, /*index=5*/f32[16,128]{1,0:T(8,128)S(1)}) fusion(f32[16,128]{1,0:T(8,128)S(1)} %get-tuple-element.399, f32[16,128]{1,0:T(8,128)S(1)} %get-tuple-element.401, ...), kind=kLoop, calls=%fused_computation.63.clone.1 | loop fusion | flops 11784192 | bytes 196608 | tf_op jit(solution)/shard_map/while/body/eval_jaxpr/reduce_sum | solution.py:38
  134.7 4.5 %fusion.68 = (f32[16,128]{1,0:T(8,128)S(1)}, f32[16,128]{1,0:T(8,128)S(1)}, f32[16,128]{1,0:T(8,128)S(1)}, f32[16,128]{1,0:T(8,128)S(1)}, f32[16,128]{1,0:T(8,128)S(1)}, /*index=5*/f32[16,128]{1,0:T(8,128)S(1)}) fusion(f32[16,128]{1,0:T(8,128)S(1)} %get-tuple-element.399, f32[16,128]{1,0:T(8,128)S(1)} %get-tuple-element.401, ...), kind=kLoop, calls=%fused_computation.63.clone.1 | loop fusion | flops 11784192 | bytes 196608 | tf_op jit(solution)/shard_map/while/body/eval_jaxpr/reduce_sum | solution.py:38
  144.6 4.5 %fusion.68 = (f32[16,128]{1,0:T(8,128)S(1)}, f32[16,128]{1,0:T(8,128)S(1)}, f32[16,128]{1,0:T(8,128)S(1)}, f32[16,128]{1,0:T(8,128)S(1)}, f32[16,128]{1,0:T(8,128)S(1)}, /*index=5*/f32[16,128]{1,0:T(8,128)S(1)}) fusion(f32[16,128]{1,0:T(8,128)S(1)} %get-tuple-element.399, f32[16,128]{1,0:T(8,128)S(1)} %get-tuple-element.401, ...), kind=kLoop, calls=%fused_computation.63.clone.1 | loop fusion | flops 11784192 | bytes 196608 | tf_op jit(solution)/shard_map/while/body/eval_jaxpr/reduce_sum | solution.py:38
  154.6 4.5 %fusion.68 = (f32[16,128]{1,0:T(8,128)S(1)}, f32[16,128]{1,0:T(8,128)S(1)}, f32[16,128]{1,0:T(8,128)S(1)}, f32[16,128]{1,0:T(8,128)S(1)}, f32[16,128]{1,0:T(8,128)S(1)}, /*index=5*/f32[16,128]{1,0:T(8,128)S(1)}) fusion(f32[16,128]{1,0:T(8,128)S(1)} %get-tuple-element.399, f32[16,128]{1,0:T(8,128)S(1)} %get-tuple-element.401, ...), kind=kLoop, calls=%fused_computation.63.clone.1 | loop fusion | flops 11784192 | bytes 196608 | tf_op jit(solution)/shard_map/while/body/eval_jaxpr/reduce_sum | solution.py:38
  164.5 4.5 %fusion.68 = (f32[16,128]{1,0:T(8,128)S(1)}, f32[16,128]{1,0:T(8,128)S(1)}, f32[16,128]{1,0:T(8,128)S(1)}, f32[16,128]{1,0:T(8,128)S(1)}, f32[16,128]{1,0:T(8,128)S(1)}, /*index=5*/f32[16,128]{1,0:T(8,128)S(1)}) fusion(f32[16,128]{1,0:T(8,128)S(1)} %get-tuple-element.399, f32[16,128]{1,0:T(8,128)S(1)} %get-tuple-element.401, ...), kind=kLoop, calls=%fused_computation.63.clone.1 | loop fusion | flops 11784192 | bytes 196608 | tf_op jit(solution)/shard_map/while/body/eval_jaxpr/reduce_sum | solution.py:38
  174.4 4.5 %fusion.68 = (f32[16,128]{1,0:T(8,128)S(1)}, f32[16,128]{1,0:T(8,128)S(1)}, f32[16,128]{1,0:T(8,128)S(1)}, f32[16,128]{1,0:T(8,128)S(1)}, f32[16,128]{1,0:T(8,128)S(1)}, /*index=5*/f32[16,128]{1,0:T(8,128)S(1)}) fusion(f32[16,128]{1,0:T(8,128)S(1)} %get-tuple-element.399, f32[16,128]{1,0:T(8,128)S(1)} %get-tuple-element.401, ...), kind=kLoop, calls=%fused_computation.63.clone.1 | loop fusion | flops 11784192 | bytes 196608 | tf_op jit(solution)/shard_map/while/body/eval_jaxpr/reduce_sum | solution.py:38
  184.4 4.5 %fusion.68 = (f32[16,128]{1,0:T(8,128)S(1)}, f32[16,128]{1,0:T(8,128)S(1)}, f32[16,128]{1,0:T(8,128)S(1)}, f32[16,128]{1,0:T(8,128)S(1)}, f32[16,128]{1,0:T(8,128)S(1)}, /*index=5*/f32[16,128]{1,0:T(8,128)S(1)}) fusion(f32[16,128]{1,0:T(8,128)S(1)} %get-tuple-element.399, f32[16,128]{1,0:T(8,128)S(1)} %get-tuple-element.401, ...), kind=kLoop, calls=%fused_computation.63.clone.1 | loop fusion | flops 11784192 | bytes 196608 | tf_op jit(solution)/shard_map/while/body/eval_jaxpr/reduce_sum | solution.py:38
  194.3 4.5 %fusion.68 = (f32[16,128]{1,0:T(8,128)S(1)}, f32[16,128]{1,0:T(8,128)S(1)}, f32[16,128]{1,0:T(8,128)S(1)}, f32[16,128]{1,0:T(8,128)S(1)}, f32[16,128]{1,0:T(8,128)S(1)}, /*index=5*/f32[16,128]{1,0:T(8,128)S(1)}) fusion(f32[16,128]{1,0:T(8,128)S(1)} %get-tuple-element.399, f32[16,128]{1,0:T(8,128)S(1)} %get-tuple-element.401, ...), kind=kLoop, calls=%fused_computation.63.clone.1 | loop fusion | flops 11784192 | bytes 196608 | tf_op jit(solution)/shard_map/while/body/eval_jaxpr/reduce_sum | solution.py:38
  204.3 4.5 %fusion.68 = (f32[16,128]{1,0:T(8,128)S(1)}, f32[16,128]{1,0:T(8,128)S(1)}, f32[16,128]{1,0:T(8,128)S(1)}, f32[16,128]{1,0:T(8,128)S(1)}, f32[16,128]{1,0:T(8,128)S(1)}, /*index=5*/f32[16,128]{1,0:T(8,128)S(1)}) fusion(f32[16,128]{1,0:T(8,128)S(1)} %get-tuple-element.399, f32[16,128]{1,0:T(8,128)S(1)} %get-tuple-element.401, ...), kind=kLoop, calls=%fused_computation.63.clone.1 | loop fusion | flops 11784192 | bytes 196608 | tf_op jit(solution)/shard_map/while/body/eval_jaxpr/reduce_sum | solution.py:38
  214.2 4.5 %fusion.68 = (f32[16,128]{1,0:T(8,128)S(1)}, f32[16,128]{1,0:T(8,128)S(1)}, f32[16,128]{1,0:T(8,128)S(1)}, f32[16,128]{1,0:T(8,128)S(1)}, f32[16,128]{1,0:T(8,128)S(1)}, /*index=5*/f32[16,128]{1,0:T(8,128)S(1)}) fusion(f32[16,128]{1,0:T(8,128)S(1)} %get-tuple-element.399, f32[16,128]{1,0:T(8,128)S(1)} %get-tuple-element.401, ...), kind=kLoop, calls=%fused_computation.63.clone.1 | loop fusion | flops 11784192 | bytes 196608 | tf_op jit(solution)/shard_map/while/body/eval_jaxpr/reduce_sum | solution.py:38
  224.2 4.5 %fusion.68 = (f32[16,128]{1,0:T(8,128)S(1)}, f32[16,128]{1,0:T(8,128)S(1)}, f32[16,128]{1,0:T(8,128)S(1)}, f32[16,128]{1,0:T(8,128)S(1)}, f32[16,128]{1,0:T(8,128)S(1)}, /*index=5*/f32[16,128]{1,0:T(8,128)S(1)}) fusion(f32[16,128]{1,0:T(8,128)S(1)} %get-tuple-element.399, f32[16,128]{1,0:T(8,128)S(1)} %get-tuple-element.401, ...), kind=kLoop, calls=%fused_computation.63.clone.1 | loop fusion | flops 11784192 | bytes 196608 | tf_op jit(solution)/shard_map/while/body/eval_jaxpr/reduce_sum | solution.py:38
  234.1 4.5 %fusion.68 = (f32[16,128]{1,0:T(8,128)S(1)}, f32[16,128]{1,0:T(8,128)S(1)}, f32[16,128]{1,0:T(8,128)S(1)}, f32[16,128]{1,0:T(8,128)S(1)}, f32[16,128]{1,0:T(8,128)S(1)}, /*index=5*/f32[16,128]{1,0:T(8,128)S(1)}) fusion(f32[16,128]{1,0:T(8,128)S(1)} %get-tuple-element.399, f32[16,128]{1,0:T(8,128)S(1)} %get-tuple-element.401, ...), kind=kLoop, calls=%fused_computation.63.clone.1 | loop fusion | flops 11784192 | bytes 196608 | tf_op jit(solution)/shard_map/while/body/eval_jaxpr/reduce_sum | solution.py:38
  244.1 4.5 %fusion.68 = (f32[16,128]{1,0:T(8,128)S(1)}, f32[16,128]{1,0:T(8,128)S(1)}, f32[16,128]{1,0:T(8,128)S(1)}, f32[16,128]{1,0:T(8,128)S(1)}, f32[16,128]{1,0:T(8,128)S(1)}, /*index=5*/f32[16,128]{1,0:T(8,128)S(1)}) fusion(f32[16,128]{1,0:T(8,128)S(1)} %get-tuple-element.399, f32[16,128]{1,0:T(8,128)S(1)} %get-tuple-element.401, ...), kind=kLoop, calls=%fused_computation.63.clone.1 | loop fusion | flops 11784192 | bytes 196608 | tf_op jit(solution)/shard_map/while/body/eval_jaxpr/reduce_sum | solution.py:38
  254.0 4.5 %fusion.68 = (f32[16,128]{1,0:T(8,128)S(1)}, f32[16,128]{1,0:T(8,128)S(1)}, f32[16,128]{1,0:T(8,128)S(1)}, f32[16,128]{1,0:T(8,128)S(1)}, f32[16,128]{1,0:T(8,128)S(1)}, /*index=5*/f32[16,128]{1,0:T(8,128)S(1)}) fusion(f32[16,128]{1,0:T(8,128)S(1)} %get-tuple-element.399, f32[16,128]{1,0:T(8,128)S(1)} %get-tuple-element.401, ...), kind=kLoop, calls=%fused_computation.63.clone.1 | loop fusion | flops 11784192 | bytes 196608 | tf_op jit(solution)/shard_map/while/body/eval_jaxpr/reduce_sum | solution.py:38
  264.0 4.5 %fusion.68 = (f32[16,128]{1,0:T(8,128)S(1)}, f32[16,128]{1,0:T(8,128)S(1)}, f32[16,128]{1,0:T(8,128)S(1)}, f32[16,128]{1,0:T(8,128)S(1)}, f32[16,128]{1,0:T(8,128)S(1)}, /*index=5*/f32[16,128]{1,0:T(8,128)S(1)}) fusion(f32[16,128]{1,0:T(8,128)S(1)} %get-tuple-element.399, f32[16,128]{1,0:T(8,128)S(1)} %get-tuple-element.401, ...), kind=kLoop, calls=%fused_computation.63.clone.1 | loop fusion | flops 11784192 | bytes 196608 | tf_op jit(solution)/shard_map/while/body/eval_jaxpr/reduce_sum | solution.py:38
  273.9 4.5 %fusion.68 = (f32[16,128]{1,0:T(8,128)S(1)}, f32[16,128]{1,0:T(8,128)S(1)}, f32[16,128]{1,0:T(8,128)S(1)}, f32[16,128]{1,0:T(8,128)S(1)}, f32[16,128]{1,0:T(8,128)S(1)}, /*index=5*/f32[16,128]{1,0:T(8,128)S(1)}) fusion(f32[16,128]{1,0:T(8,128)S(1)} %get-tuple-element.399, f32[16,128]{1,0:T(8,128)S(1)} %get-tuple-element.401, ...), kind=kLoop, calls=%fused_computation.63.clone.1 | loop fusion | flops 11784192 | bytes 196608 | tf_op jit(solution)/shard_map/while/body/eval_jaxpr/reduce_sum | solution.py:38
  279.2 2.7 scatter_custom_fusion
  281.9 3.4 scatter_custom_fusion.1
  287.8 6.1 %all-to-all-start.2 = ((f32[128,4,384]{2,1,0:T(4,128)}), f32[128,4,384]{2,1,0:T(4,128)S(1)}, u32[]{:S(2)}, u32[]{:S(2)}) async-start(f32[128,4,384]{2,1,0:T(4,128)} %reshape.364), calls=%async_computation.2 | async-start | bytes 1572864 | tf_op jit(solution)/shard_map/all_to_all | solution.py:120
  293.9 122.2 %while.25 = (s32[]{:T(128)}, f32[16,32,384]{2,1,0:T(8,128)}, f32[16,32,768]{2,1,0:T(8,128)S(1)}, f32[64,3,3]{0,2,1:T(4,128)S(1)}, f32[16,32,384]{2,1,0:T(8,128)}, /*index=5*/s32[]{:T(128)}) while((s32[]{:T(128)}, f32[16,32,384]{2,1,0:T(8,128)}, f32[16,32,768]{2,1,0:T(8,128)S(1)}, f32[64,3,3]{0,2,1:T(4,128)S(1)}, f32[16,32,384]{2,1,0:T(8,128)}, ...), condition=%wide.region_14.15_spmd, body=%wide.region_10.14_spmd.sunk | while | flops 31472320 | bytes 1197901 | solution.py:130
  294.8 2.0 fusion.61
  296.8 2.0 fusion.60
  302.4 2.0 fusion.61
  310.1 2.0 fusion.61
  312.1 2.0 fusion.60
  317.7 2.0 fusion.61
  325.3 2.0 fusion.61
  333.0 2.0 fusion.61
  340.6 2.0 fusion.61
  348.2 2.0 fusion.61
  350.3 2.0 fusion.60
  355.9 2.0 fusion.61
  363.5 2.0 fusion.61
  371.1 2.0 fusion.61
  378.8 2.0 fusion.61
  386.4 2.0 fusion.61
  394.0 2.0 fusion.61
  401.7 2.0 fusion.61
  409.3 2.0 fusion.61
  416.5 5.7 %scatter_custom_fusion.2 = f32[512,384]{1,0:T(8,128)} fusion(f32[512,384]{1,0:T(8,128)} %bitcast.118, s32[512]{0:T(512)S(1)} %reshape.435, f32[512,384]{1,0:T(8,128)S(1)} %reshape.365, f32[512]{0:T(512)S(1)} %reshape.368), kind=kCustom, calls=%fused_computation.85 | custom fusion | flops 393216 | bytes 1574912 | tf_op jit(solution)/shard_map/scatter-add | solution.py:128
  (466 shorter events, 180.7 us)
Async XLA Ops:
  4.9 13.0 %copy-start = (f32[512,768]{1,0:T(8,128)S(1)}, f32[512,768]{1,0:T(8,128)}, u32[]{:S(2)}) copy-start(f32[512,768]{1,0:T(8,128)} %param.10) | copy-start | bytes 4718596
  6.0 28.0 %all-to-all-start.1 = ((f32[128,4,384]{2,1,0:T(4,128)}), f32[128,4,384]{2,1,0:T(4,128)}, u32[]{:S(2)}, u32[]{:S(2)}) async-start(f32[128,4,384]{2,1,0:T(4,128)} %broadcast_multiply_fusion.1), calls=%async_computation.1 | async-start | bytes 1572864 | tf_op jit(solution)/shard_map/all_to_all | solution.py:77
  34.0 84.2 %all-to-all-start = ((f32[128,4,768]{2,1,0:T(4,128)}), f32[128,4,768]{2,1,0:T(4,128)}, u32[]{:S(2)}, u32[]{:S(2)}) async-start(f32[128,4,768]{2,1,0:T(4,128)} %broadcast_multiply_fusion), calls=%async_computation | async-start | bytes 3145728 | tf_op jit(solution)/shard_map/all_to_all | solution.py:78
  39.6 0.8 copy-start.2
  39.7 76.0 %copy-start.1 = (s32[256,2]{0,1:T(2,128)S(1)}, s32[256,2]{0,1:T(2,128)}, u32[]{:S(2)}) copy-start(s32[256,2]{0,1:T(2,128)} %param.12) | copy-start | bytes 6148
  287.8 128.5 %all-to-all-start.2 = ((f32[128,4,384]{2,1,0:T(4,128)}), f32[128,4,384]{2,1,0:T(4,128)S(1)}, u32[]{:S(2)}, u32[]{:S(2)}) async-start(f32[128,4,384]{2,1,0:T(4,128)} %reshape.364), calls=%async_computation.2 | async-start | bytes 1572864 | tf_op jit(solution)/shard_map/all_to_all | solution.py:120
where the time goes:
time: 425 us; the launch traced here: 422 us
  other arithmetic  209 us (49%)
  local copies, waits for them, and re-layouts  101 us (24%)
  blocking collectives  74.9 us (18%)
  starting transfers between devices  23.6 us (6%)
  waiting for transfers between devices  10.2 us (2%)
    reduce_sum x48, other arithmetic, far_tile(): jnp.sum(weight * offsets[index], axis=1)  97.1 us
    psum x1, blocking collectives, on_device(): total_moments = lax.psum(local_moments, ('gx', 'yz'))  74.9 us
    reduce_sum x16, other arithmetic, pair_tile(): jnp.sum(weight * offsets[index], axis=1)  71.9 us
    gather x16, local copies, waits for them, and re-layouts, pair_block(): recv_pos[ids_group[:, 1]]  27.5 us
    gather x16, local copies, waits for them, and re-layouts, pair_block(): recv_pos[ids_group[:, 0]]  27.5 us
    squeeze x32, local copies, waits for them, and re-layouts, on_device(): lax.map(lambda packed: far_tile(packed[0], packed[1], moments, width), (p...  13 us
    all_to_all x1, starting transfers between devices, on_device(): lax.all_to_all(out_pos, ('gx', 'yz'), split_axis=0, concat_axis=0, tiled=...  11.9 us
    dynamic_update_slice x16, other arithmetic, on_device(): lax.map(pair_block, (pair_ids.reshape(-1, group_size, 2), usable.reshape(...  11.2 us
  transfers between devices with their start and end apart: 3, of which 1 were waited for; matrix products, arithmetic and copies ran while one was open for 31% of the time, Pallas kernels for 0%

commit v1 on v0

v1 whole, which is shorter than its diff:
```python
import math

import jax
import jax.numpy as jnp
from jax import lax
from jax.experimental import pallas as pl
from jax.experimental.pallas import tpu as pltpu
from jax.sharding import PartitionSpec as P

MESH = pl.DeviceIdType.MESH
F32 = jnp.float32
BF16 = jnp.bfloat16
KC = 64
WIDTH = 128
MIDDLE = 2.0
ROWS = 16
UNROLL = 4
VMEM_LIMIT = 50 * 2**20


def high_low(value):
    high = value.astype(BF16)
    return high, (value - high.astype(F32)).astype(BF16)


def features(place, tensor):
    scale = WIDTH**-0.25
    rows = [scale * math.sqrt(1.5) * tensor[k][k] for k in range(3)]
    for k, l in ((0, 1), (0, 2), (1, 2)):
        rows.append(scale * math.sqrt(0.75) * (tensor[k][l] + tensor[l][k]))
        rows.append(scale * 0.5 * (tensor[k][l] - tensor[l][k]))
    square = place[0] * place[0] + place[1] * place[1] + place[2] * place[2] + 0.125
    upper = square.astype(BF16).astype(F32)
    one = jnp.ones_like(square)
    return rows + list(place) + [upper, square - upper, one, one]


def pack_kernel(ids_ref, pos_ref, vec_ref, send_ref, base_ref, packed):
    def group(step, carry):
        rows = pl.ds(pl.multiple_of(step * 8, 8), 8)
        place = [pos_ref[rows, pl.ds(k * WIDTH, WIDTH)] - MIDDLE for k in range(3)]
        line = [vec_ref[rows, pl.ds(k * WIDTH, WIDTH)] for k in range(3)]
        burg = [vec_ref[rows, pl.ds((3 + k) * WIDTH, WIDTH)] for k in range(3)]
        for row, value in enumerate(features(place, [[b * l for l in line] for b in burg])):
            base_ref[pl.ds(step * 8 * ROWS + row, 8, stride=ROWS), :] = value
        square = line[0] * line[0] + line[1] * line[1] + line[2] * line[2]
        inverse = lax.rsqrt(jnp.maximum(square, 1e-36))
        side = jnp.where(line[2] < 0, -inverse, inverse)
        length = square * side
        tilt = 1.0 / (1.0 + line[2] * side)
        out = place + [b * length for b in burg] + [line[0] * side * tilt, line[1] * side * tilt]
        for row, value in enumerate(out):
            packed[pl.ds(step * 64 + row, 8, stride=8), :] = value
        return carry

    lax.fori_loop(0, pos_ref.shape[0] // 8, group, 0)

    def pick(step, carry):
        for part in range(8):
            slot = step * 8 + part
            source = jnp.maximum(ids_ref[slot], 0) * 8
            send_ref[pl.ds(pl.multiple_of(slot * 8, 8), 8), :] = packed[
                pl.ds(pl.multiple_of(source, 8), 8), :
            ]
        return carry

    lax.fori_loop(0, ids_ref.shape[0] // 8, pick, 0)


def moment_kernel(size_gx, size_yz, x_ref, o_ref, near, far, total, send_sem, recv_sem):
    gx, yz = lax.axis_index("gx"), lax.axis_index("yz")
    barrier = pltpu.get_barrier_semaphore()

    def along_yz(step):
        return gx, lax.rem(yz + step, size_yz)

    def along_gx(step):
        return lax.rem(gx + step, size_gx), yz

    for step in range(1, size_yz):
        pl.semaphore_signal(barrier, inc=1, device_id=along_yz(step), device_id_type=MESH)
    for step in range(1, size_gx):
        pl.semaphore_signal(barrier, inc=1, device_id=along_gx(step), device_id_type=MESH)
    pl.semaphore_wait(barrier, size_yz + size_gx - 2)

    def exchange(source, held, other, size, sem):
        copies = [
            pltpu.make_async_remote_copy(
                src_ref=source,
                dst_ref=held.at[step],
                send_sem=send_sem.at[sem + step],
                recv_sem=recv_sem.at[sem + step],
                device_id=other(step),
                device_id_type=MESH,
            )
            for step in range(1, size)
        ]
        for copy in copies:
            copy.start()
        for copy in copies:
            copy.wait()
        result = source[...]
        for step in range(1, size):
            result = result + held[step]
        return result

    total[...] = exchange(x_ref, near, along_yz, size_yz, 0)
    o_ref[...] = exchange(total, far, along_gx, size_gx, size_yz)


def far_kernel(base_ref, left_ref, right_ref, o_ref, tile):
    left = left_ref[...]
    high, low = high_low(left)
    left = jnp.concatenate([high, high, low], axis=1)
    right = right_ref[...].astype(BF16)
    right = jnp.concatenate([right, right], axis=1)

    def pair(step, carry):
        for part in range(4):
            at = step * 8 + part * 2
            first = base_ref[pl.ds(pl.multiple_of(at * ROWS, ROWS), ROWS), :]
            second = base_ref[pl.ds(pl.multiple_of(at * ROWS + ROWS, ROWS), ROWS), :]
            both = jnp.concatenate([first, second], axis=1)
            high, low = high_low(both)
            forms = jnp.dot(
                left, jnp.concatenate([high, low, high], axis=0), preferred_element_type=F32
            )
            root = lax.rsqrt(forms[KC:])
            weight = forms[:KC] * root * (root * root)
            high, low = high_low(weight)
            sums = jnp.dot(
                right, jnp.concatenate([high, low], axis=0), preferred_element_type=F32
            )
            force = both[8:] * sums[6:7] - sums[:8]
            tile[pl.ds(part * 16, 8), :] = force[:, :WIDTH]
            tile[pl.ds(part * 16 + 8, 8), :] = force[:, WIDTH:]
        for k in range(3):
            o_ref[pl.ds(pl.multiple_of(step * 8, 8), 8), pl.ds(k * WIDTH, WIDTH)] = tile[
                pl.ds(1 + k, 8, stride=8), :
            ]
        return carry

    lax.fori_loop(0, o_ref.shape[0] // 8, pair, 0)


def near_kernel(live_ref, pairs_ref, recv_ref, o_ref, base, total):
    slots = o_ref.shape[0]

    def group(step, carry):
        got = [recv_ref[pl.ds(step * 64 + row, 8, stride=8), :] for row in range(8)]
        square = got[6] * got[6] + got[7] * got[7]
        inverse = 1.0 / (1.0 + square)
        line = [2.0 * got[6] * inverse, 2.0 * got[7] * inverse, (1.0 - square) * inverse]
        for row, value in enumerate(
            features(got[:3], [[b * l for l in line] for b in got[3:6]])
        ):
            base[pl.ds(step * 8 * ROWS + row, 8, stride=ROWS), :] = value
        total[pl.ds(pl.multiple_of(step * 64, 64), 64), :] = jnp.zeros((64, WIDTH), F32)
        return carry

    lax.fori_loop(0, slots // 8, group, 0)
    row = lax.broadcasted_iota(jnp.int32, (8, WIDTH), 0)
    zero = jnp.zeros((8, WIDTH), F32)

    def one_pair(first, second):
        tile_a = base[pl.ds(pl.multiple_of(first * ROWS, ROWS), ROWS), :]
        tile_b = base[pl.ds(pl.multiple_of(second * ROWS, ROWS), ROWS), :]
        high_a, low_a = high_low(tile_a)
        left = jnp.concatenate([high_a, high_a, low_a, low_a], axis=0)
        last = tile_b[8:]
        turned = pltpu.roll(last, 2, 0)
        squares = jnp.where(
            row >= 6, turned, jnp.where(row >= 4, 1.0, jnp.where(row >= 1, -2.0 * last, 0.0))
        )
        couplings = jnp.concatenate([tile_b[:8], jnp.where(row == 0, last, 0.0)], axis=0)
        high, low = high_low(
            jnp.concatenate([couplings, jnp.concatenate([zero, squares], axis=0)], axis=1)
        )
        forms = lax.dot_general(
            left,
            jnp.concatenate([high, low, high, low], axis=0),
            (((0,), (0,)), ((), ())),
            preferred_element_type=F32,
        )
        root = lax.rsqrt(forms[:, WIDTH:])
        weight = forms[:, :WIDTH] * root * (root * root)
        high, low = high_low(weight)

        def places(tile):
            value = jnp.concatenate(high_low(tile[8:]), axis=0)
            return jnp.concatenate([value, value], axis=1)

        on_b = jnp.dot(
            places(tile_a), jnp.concatenate([high, low], axis=0), preferred_element_type=F32
        )
        on_a = lax.dot_general(
            places(tile_b),
            jnp.concatenate([high, low], axis=1),
            (((1,), (1,)), ((), ())),
            preferred_element_type=F32,
        )
        return [
            tile[8:] * sums[6:7] - (sums[:8] + sums[8:])
            for tile, sums in ((tile_a, on_a), (tile_b, on_b))
        ]

    def step_pairs(step, carry):
        done = []
        for part in range(UNROLL):
            at = (step * UNROLL + part) * 2
            ids = [pairs_ref[at], pairs_ref[at + 1]]
            forces = one_pair(jnp.maximum(ids[0], 0), jnp.maximum(ids[1], 0))
            done += [(jnp.where(i < 0, slots, i), force) for i, force in zip(ids, forces)]
        for i, force in done:
            place = pl.ds(pl.multiple_of(i * 8, 8), 8)
            total[place, :] = total[place, :] + force
        return carry

    lax.fori_loop(0, (live_ref[0] + UNROLL - 1) // UNROLL, step_pairs, 0)

    def finish(step, carry):
        for k in range(3):
            o_ref[pl.ds(pl.multiple_of(step * 8, 8), 8), pl.ds(k * WIDTH, WIDTH)] = total[
                pl.ds(step * 64 + 1 + k, 8, stride=8), :
            ]
        return carry

    lax.fori_loop(0, slots // 8, finish, 0)


def final_kernel(ids_ref, got_ref, far_ref, o_ref):
    blocks, slots = o_ref.shape[0], got_ref.shape[0]
    high, low = high_low(got_ref[...])
    chunk = 128

    def part(step, carry):
        rows = pl.ds(pl.multiple_of(step * chunk, chunk), chunk)
        index = lax.broadcasted_iota(jnp.int32, (chunk, slots), 0) + step * chunk
        chosen = jnp.where(index == ids_ref[...], 1.0, 0.0).astype(BF16)
        o_ref[rows, :] = (
            far_ref[rows, :]
            + jnp.dot(chosen, high, preferred_element_type=F32)
            + jnp.dot(chosen, low, preferred_element_type=F32)
        )
        return carry

    lax.fori_loop(0, blocks // chunk, part, 0)


VM = pl.BlockSpec(memory_space=pltpu.VMEM)
SM = pl.BlockSpec(memory_space=pltpu.SMEM)


def call(kernel, name, outs, in_specs, scratch, args, cost=None, **params):
    return pl.pallas_call(
        kernel,
        name=name,
        out_shape=outs,
        in_specs=in_specs,
        out_specs=jax.tree.map(lambda _: VM, outs),
        scratch_shapes=scratch,
        cost_estimate=cost,
        compiler_params=pltpu.CompilerParams(vmem_limit_bytes=VMEM_LIMIT, **params),
    )(*args)


def array(*shape):
    return jax.ShapeDtypeStruct(shape, F32)


def far_sides(moments):
    scale = WIDTH**-0.25
    m = moments.reshape(KC, 3, 3)
    rows = [m[:, k, k] / (scale * math.sqrt(1.5)) for k in range(3)]
    for k, l in ((0, 1), (0, 2), (1, 2)):
        rows.append((m[:, k, l] + m[:, l, k]) / (2.0 * scale * math.sqrt(0.75)))
        rows.append((m[:, k, l] - m[:, l, k]) / scale)
    strength = jnp.pad(jnp.stack(rows, axis=1) / math.sqrt(KC), ((0, 0), (0, 7)))
    cell = jnp.arange(KC)
    centers = [(c + (0.5 - MIDDLE)).astype(F32) for c in (cell // 16, cell // 4 % 4, cell % 4)]
    one = jnp.ones((KC,), F32)
    square = sum(c * c for c in centers) + (1.0 - 0.125)
    zero = jnp.zeros((KC,), F32)
    squares = [zero] * 9 + [-2.0 * c for c in centers] + [one, one, square, zero]
    left = jnp.concatenate([strength, jnp.stack(squares, axis=1)], axis=0)
    right = [zero] + centers + [zero, zero, one, zero] + [zero] * 8
    return left, jnp.stack(right, axis=0)


def on_device(positions, vectors, send_slots, pairs, coarse):
    size_gx, size_yz = lax.axis_size("gx"), lax.axis_size("yz")
    devices = size_gx * size_yz
    blocks = positions.shape[0]
    capacity = send_slots.shape[2]
    slots = devices * capacity
    ids = send_slots.reshape(slots)
    axes = ("gx", "yz")

    send, base = call(
        pack_kernel,
        "pack",
        (array(slots * 8, WIDTH), array(blocks * ROWS, WIDTH)),
        [SM, VM, VM],
        [pltpu.VMEM((blocks * 8, WIDTH), F32)],
        (ids, positions, vectors),
    )
    got = lax.all_to_all(
        send.reshape(devices, capacity * 8, WIDTH), axes, split_axis=0, concat_axis=0, tiled=True
    ).reshape(slots * 8, WIDTH)

    parts = [vectors[:, k * WIDTH : (k + 1) * WIDTH] for k in range(6)]
    per_block = jnp.stack(
        [jnp.sum(parts[3 + k] * parts[l], axis=1) for k in range(3) for l in range(3)], axis=1
    )
    one_hot = (coarse[:, None] == jnp.arange(KC)[None, :]).astype(F32)
    local = jnp.dot(one_hot.T, per_block, precision=lax.Precision.HIGHEST)
    local = jnp.pad(local.reshape(KC * 9), (0, 1024 - KC * 9)).reshape(8, WIDTH)
    moments = call(
        lambda *refs: moment_kernel(size_gx, size_yz, *refs),
        "moments",
        array(8, WIDTH),
        [VM],
        [
            pltpu.VMEM((size_yz, 8, WIDTH), F32),
            pltpu.VMEM((size_gx, 8, WIDTH), F32),
            pltpu.VMEM((8, WIDTH), F32),
            pltpu.SemaphoreType.DMA((size_yz + size_gx,)),
            pltpu.SemaphoreType.DMA((size_yz + size_gx,)),
        ],
        (local,),
        collective_id=0,
        has_side_effects=True,
    )
    moments = moments.reshape(1024)[: KC * 9] / math.sqrt(blocks * devices * WIDTH / KC)
    far = call(
        far_kernel,
        "far",
        array(blocks, 3 * WIDTH),
        [VM, VM, VM],
        [pltpu.VMEM((64, WIDTH), F32)],
        (base, *far_sides(moments)),
        cost=pl.CostEstimate(flops=10**9, bytes_accessed=5 * 10**6, transcendentals=4 * 10**6),
    )
    live = jnp.sum((pairs[:, 0] >= 0).astype(jnp.int32)).reshape(1)
    partial_sums = call(
        near_kernel,
        "near",
        array(slots, 3 * WIDTH),
        [SM, SM, VM],
        [pltpu.VMEM((slots * ROWS, WIDTH), F32), pltpu.VMEM((slots * 8 + 8, WIDTH), F32)],
        (live, pairs.reshape(-1), got),
    )
    returned = lax.all_to_all(
        partial_sums.reshape(devices, capacity, 3 * WIDTH),
        axes,
        split_axis=0,
        concat_axis=0,
        tiled=True,
    ).reshape(slots, 3 * WIDTH)
    return call(
        final_kernel,
        "final",
        array(blocks, 3 * WIDTH),
        [VM, VM, VM],
        [],
        (ids.reshape(1, slots), returned, far),
    )


def solution(mesh):
    placed = (
        P(("gx", "yz"), None),
        P(("gx", "yz"), None),
        P(("gx", "yz"), None, None),
        P(("gx", "yz"), None),
        P(("gx", "yz")),
    )
    return jax.shard_map(
        on_device, mesh=mesh, in_specs=placed, out_specs=P(("gx", "yz"), None), check_vma=False
    )
```

time: 425 us -> 179 us (0.42)
  other arithmetic: 209 us -> 4.82 us
  Pallas kernels: 0 us -> 128 us
  local copies, waits for them, and re-layouts: 101 us -> 5.94 us
  blocking collectives: 74.9 us -> 0 us
  starting transfers between devices: 23.6 us -> 39.4 us
  waiting for transfers between devices: 10.2 us -> 0.01 us
    reduce_sum x65 -> x2, other arithmetic: 170 us -> 2.69 us  [the longest x1 2.06 us: on_device(): jnp.sum(parts[3 + k] * parts[l], axis=1)]
    pallas_call x0 -> x5, Pallas kernels: none -> 128 us  [call(): pl.pallas_call(kernel, name=name, out_shape=outs, in_specs=in_specs, out_...]
    gather x68 -> x0, local copies, waits for them, and re-layouts: 81.2 us -> none  [the longest x16 27.5 us: pair_block(): recv_pos[ids_group[:, 1]]]
    psum x1 -> x0, blocking collectives: 74.9 us -> none  [on_device(): total_moments = lax.psum(local_moments, ('gx', 'yz'))]
    dynamic_update_slice x32 -> x0, other arithmetic: 21.3 us -> none  [the longest x16 11.2 us: on_device(): lax.map(pair_block, (pair_ids.reshape(-1, group_size, 2), usable.reshape(...]
    all_to_all x3 -> x2, starting transfers between devices: 23.6 us -> 39.4 us  [the longest x1 27.9 us: on_device(): lax.all_to_all(partial_sums.reshape(devices, capacity, 3 * WIDTH), axes,...]
    squeeze x32 -> x0, local copies, waits for them, and re-layouts: 13 us -> none  [on_device(): lax.map(lambda packed: far_tile(packed[0], packed[1], moments, width), (p...]
    scatter-add x3 -> x0, other arithmetic: 11.9 us -> none  [the longest x1 5.69 us: on_device(): jax.ops.segment_sum(returned, slot_ids.reshape(-1), num_segments=blocks_h...]
  transfers between devices with their start and end apart: 3 -> 2, of which waited for: 1 -> 0; matrix products, arithmetic and copies ran while one was open for 31% -> 4% of each run, Pallas kernels for 0% -> 48%
where the time goes in v1:
time: 179 us
  Pallas kernels  128 us (72%)
  starting transfers between devices  39.4 us (22%)
  local copies, waits for them, and re-layouts  5.94 us (3%)
  other arithmetic  4.82 us (3%)
    pallas_call x5, Pallas kernels, call(): pl.pallas_call(kernel, name=name, out_shape=outs, in_specs=in_specs, out_...  128 us
    all_to_all x1, starting transfers between devices, on_device(): lax.all_to_all(partial_sums.reshape(devices, capacity, 3 * WIDTH), axes,...  27.9 us
    all_to_all x1, starting transfers between devices, on_device(): lax.all_to_all(send.reshape(devices, capacity * 8, WIDTH), axes, split_ax...  11.5 us
  transfers between devices with their start and end apart: 2, of which 0 were waited for; matrix products, arithmetic and copies ran while one was open for 4% of the time, Pallas kernels for 48%

profile of v1, /device:TPU:1, one launch (start us, length us, event | category | flops | bytes accessed | tf_op | source)
XLA Modules:
  0.0 178.6 jit_solution(12717120245789949737)
XLA Ops:
  0.0 0.8 copy.42
  0.8 0.1 reshape.494.ids_ref
  0.9 0.0 copy-start
  0.9 1.4 copy-done
  2.3 0.0 copy-start.1
  2.3 1.1 copy-done.1
  3.4 6.8 %pack.1 = (f32[4096,128]{1,0:T(8,128)}, f32[8192,128]{1,0:T(8,128)}) custom-call(s32[512]{0:T(512)S(1)} %reshape.494.ids_ref, f32[512,384]{1,0:T(8,128)S(1)} %copy-done.1, f32[512,768]{1,0:T(8,128)S(1)} %copy-done), custom_call_target="tpu_custom_call" | custom-call | tf_op jit(solution)/shard_map/pack/pallas_call | solution.py:255
  10.2 0.0 copy-start.3
  10.2 0.0 copy-start.2
  10.2 11.5 %all-to-all-start = ((f32[128,32,128]{2,1,0:T(8,128)}), f32[128,32,128]{2,1,0:T(8,128)S(1)}, u32[]{:S(2)}, u32[]{:S(2)}) async-start(f32[128,32,128]{2,1,0:T(8,128)} %bitcast.27), calls=%async_computation | async-start | bytes 4194304 | tf_op jit(solution)/shard_map/all_to_all | solution.py:307
  21.7 0.1 reshape_reshape.3.ids_ref
  21.8 2.1 %multiply_reduce_fusion = (f32[512]{0:T(512)S(1)}, f32[512]{0:T(512)S(1)}, f32[512]{0:T(512)S(1)}, f32[512]{0:T(512)S(1)}, f32[512]{0:T(512)S(1)}, /*index=5*/f3...) fusion(f32[512,768]{1,0:T(8,128)} %vec_ref.1), kind=kLoop, calls=%fused_computation | loop fusion | flops 1175040 | bytes 1591296 | tf_op jit(solution)/shard_map/reduce_sum | solution.py:313
  23.9 0.1 stack.76
  23.9 0.0 copy-done.3
  23.9 0.4 fusion.1
  24.3 0.1 reshape.499
  24.5 31.2 %moments.1 = f32[8,128]{1,0:T(8,128)S(1)} custom-call(f32[8,128]{1,0:T(8,128)S(1)} %pad_bitcast_fusion.refs_0_), custom_call_target="tpu_custom_call" | custom-call | tf_op jit(solution)/shard_map/moments/pallas_call | solution.py:255
  55.7 0.2 div.87
  56.0 0.0 copy-done.2
  56.0 0.1 copy.43
  56.1 0.1 reshape.493.pairs_ref
  56.3 0.1 stack.80
  56.5 0.6 fusion.7
  57.1 0.0 all-to-all-done
  57.1 33.3 %near.1 = f32[512,384]{1,0:T(8,128)S(1)} custom-call(s32[1]{0:T(128)} %bitcast.live_ref, s32[512]{0:T(512)S(1)} %reshape.493.pairs_ref, f32[4096,128]{1,0:T(8,128)S(1)} %bitcast.25), custom_call_target="tpu_custom_call" | custom-call | tf_op jit(solution)/shard_map/near/pallas_call | solution.py:255
  90.4 1.1 reshape.497
  91.5 27.9 %all-to-all-start.1 = ((f32[128,4,384]{2,1,0:T(4,128)}), f32[128,4,384]{2,1,0:T(4,128)S(1)}, u32[]{:S(2)}, u32[]{:S(2)}) async-start(f32[128,4,384]{2,1,0:T(4,128)} %reshape.497), calls=%async_computation.1 | async-start | bytes 1572864 | tf_op jit(solution)/shard_map/all_to_all | solution.py:353
  119.4 2.0 %multiply_reduce_fusion.9 = (f32[64]{0:T(128)S(1)}, f32[64]{0:T(128)S(1)}, f32[64]{0:T(128)S(1)}, f32[64]{0:T(128)S(1)}, f32[64]{0:T(128)S(1)}, /*index=5*/f32[6...) fusion(f32[64,3,3]{2,1,0:T(4,128)S(1)} %div.87), kind=kLoop, calls=%fused_computation.16 | loop fusion | flops 960 | bytes 4608 | tf_op jit(solution)/shard_map/div | solution.py:277
  121.5 0.1 select_maximum_fusion
  121.6 0.1 copy.46.left_ref
  121.8 54.3 %far.1.far_ref = f32[512,384]{1,0:T(8,128)S(1)} custom-call(f32[8192,128]{1,0:T(8,128)} %get-tuple-element.8.base_ref, f32[128,16]{1,0:T(8,128)S(1)} %copy.46.left_ref, f32[16,64]{1,0:T(8,128)S(1)} %stack.83.right_ref), custom_call_target="tpu_custom_call" | custom-call | flops 1000000000 | bytes 5000000 | tf_op jit(solution)/shard_map/far/pallas_call | solution.py:255
  176.0 0.0 all-to-all-done.1
  176.0 0.3 reshape.498.got_ref
  176.3 2.2 %final.1 = f32[512,384]{1,0:T(8,128)} custom-call(s32[1,512]{1,0:T(1,128)S(1)} %reshape_reshape.3.ids_ref, f32[512,384]{1,0:T(8,128)S(1)} %reshape.498.got_ref, f32[512,384]{1,0:T(8,128)S(1)} %far.1.far_ref), custom_call_target="tpu_custom_call" | custom-call | tf_op jit(solution)/shard_map/final/pallas_call | solution.py:255
  (16 shorter events, 0.2 us)
Async XLA Ops:
  0.9 1.4 copy-start
  2.3 1.1 copy-start.1
  10.2 13.7 %copy-start.3 = (s32[512]{0:T(512)S(1)}, s32[512]{0:T(512)}, u32[]{:S(2)}) copy-start(s32[512]{0:T(512)} %param.9) | copy-start | bytes 6148
  10.2 45.8 %copy-start.2 = (s32[256,2]{0,1:T(2,128)S(1)}, s32[256,2]{0,1:T(2,128)}, u32[]{:S(2)}) copy-start(s32[256,2]{0,1:T(2,128)} %param.8) | copy-start | bytes 6148
  10.2 46.9 %all-to-all-start = ((f32[128,32,128]{2,1,0:T(8,128)}), f32[128,32,128]{2,1,0:T(8,128)S(1)}, u32[]{:S(2)}, u32[]{:S(2)}) async-start(f32[128,32,128]{2,1,0:T(8,128)} %bitcast.27), calls=%async_computation | async-start | bytes 4194304 | tf_op jit(solution)/shard_map/all_to_all | solution.py:307
  91.5 84.5 %all-to-all-start.1 = ((f32[128,4,384]{2,1,0:T(4,128)}), f32[128,4,384]{2,1,0:T(4,128)S(1)}, u32[]{:S(2)}, u32[]{:S(2)}) async-start(f32[128,4,384]{2,1,0:T(4,128)} %reshape.497), calls=%async_computation.1 | async-start | bytes 1572864 | tf_op jit(solution)/shard_map/all_to_all | solution.py:353

commit v2 on v1

--- a/solution.py
+++ b/solution.py
@@ -15,6 +15,7 @@
 MIDDLE = 2.0
 ROWS = 16
 UNROLL = 4
+FAR_GROUPS = 1
 VMEM_LIMIT = 50 * 2**20
 
 
@@ -108,42 +109,59 @@
     o_ref[...] = exchange(total, far, along_gx, size_gx, size_yz)
 
 
-def far_kernel(base_ref, left_ref, right_ref, o_ref, tile):
-    left = left_ref[...]
-    high, low = high_low(left)
+def far_kernel(pos_ref, base_ref, left_ref, o_ref, *tiles):
+    high, low = high_low(left_ref[...])
     left = jnp.concatenate([high, high, low], axis=1)
-    right = right_ref[...].astype(BF16)
-    right = jnp.concatenate([right, right], axis=1)
-
-    def pair(step, carry):
-        for part in range(4):
-            at = step * 8 + part * 2
-            first = base_ref[pl.ds(pl.multiple_of(at * ROWS, ROWS), ROWS), :]
-            second = base_ref[pl.ds(pl.multiple_of(at * ROWS + ROWS, ROWS), ROWS), :]
-            both = jnp.concatenate([first, second], axis=1)
-            high, low = high_low(both)
-            forms = jnp.dot(
-                left, jnp.concatenate([high, low, high], axis=0), preferred_element_type=F32
-            )
-            root = lax.rsqrt(forms[KC:])
-            weight = forms[:KC] * root * (root * root)
-            high, low = high_low(weight)
-            sums = jnp.dot(
-                right, jnp.concatenate([high, low], axis=0), preferred_element_type=F32
-            )
-            force = both[8:] * sums[6:7] - sums[:8]
-            tile[pl.ds(part * 16, 8), :] = force[:, :WIDTH]
-            tile[pl.ds(part * 16 + 8, 8), :] = force[:, WIDTH:]
-        for k in range(3):
-            o_ref[pl.ds(pl.multiple_of(step * 8, 8), 8), pl.ds(k * WIDTH, WIDTH)] = tile[
-                pl.ds(1 + k, 8, stride=8), :
-            ]
-        return carry
-
-    lax.fori_loop(0, o_ref.shape[0] // 8, pair, 0)
-
-
-def near_kernel(live_ref, pairs_ref, recv_ref, o_ref, base, total):
+
+    def group(step, carry):
+        for part in range(FAR_GROUPS):
+            far_group(step * FAR_GROUPS + part, left, pos_ref, base_ref, o_ref, tiles[part])
+        return carry
+
+    lax.fori_loop(0, o_ref.shape[0] // (8 * FAR_GROUPS), group, 0)
+
+
+def far_group(step, left, pos_ref, base_ref, o_ref, tile):
+    for part in range(4):
+        at = (step * 8 + part * 2) * ROWS
+        both = jnp.concatenate(
+            [base_ref[pl.ds(pl.multiple_of(at + i * ROWS, ROWS), ROWS), :] for i in range(2)], axis=1
+        )
+        high, low = high_low(both)
+        forms = jnp.dot(
+            left, jnp.concatenate([high, low, high], axis=0), preferred_element_type=F32
+        )
+        root = lax.rsqrt(forms[KC:])
+        weight = forms[:KC] * root * (root * root)
+        w = [weight[8 * v : 8 * v + 8] for v in range(8)]
+        s = [w[2 * i] + w[2 * i + 1] for i in range(4)]
+        sums = [
+            1.5 * (s[3] - s[0]) + 0.5 * (s[2] - s[1]),
+            (w[1] + w[3]) + (w[5] + w[7]),
+            (s[0] + s[1]) + (s[2] + s[3]),
+        ]
+        for q, value in enumerate(sums):
+            for i in range(2):
+                tile[pl.ds(q * 64 + (part * 2 + i) * 8, 8), :] = value[:, i * WIDTH : (i + 1) * WIDTH]
+    along_x, upper, t = (
+        [tile[pl.ds(q * 64 + r, 8, stride=8), :] for r in range(8)] for q in range(3)
+    )
+    first = (t[0] + t[1]) + (t[2] + t[3])
+    second = (t[4] + t[5]) + (t[6] + t[7])
+    whole = first + second
+    m = [t[i] + t[i + 4] for i in range(4)]
+    centers = [
+        sum(along_x[1:], along_x[0]),
+        2.0 * sum(upper[1:], upper[0]) - 1.5 * first - 0.5 * second,
+        1.5 * (m[3] - m[0]) + 0.5 * (m[2] - m[1]),
+    ]
+    rows = pl.ds(pl.multiple_of(step * 8, 8), 8)
+    for k in range(3):
+        column = pl.ds(k * WIDTH, WIDTH)
+        o_ref[rows, column] = (pos_ref[rows, column] - MIDDLE) * whole - centers[k]
+
+
+def near_kernel(live_ref, pairs_ref, recv_ref, o_ref, base, total, *matrices):
     slots = o_ref.shape[0]
 
     def group(step, carry):
@@ -161,10 +179,15 @@
     lax.fori_loop(0, slots // 8, group, 0)
     row = lax.broadcasted_iota(jnp.int32, (8, WIDTH), 0)
     zero = jnp.zeros((8, WIDTH), F32)
-
-    def one_pair(first, second):
-        tile_a = base[pl.ds(pl.multiple_of(first * ROWS, ROWS), ROWS), :]
-        tile_b = base[pl.ds(pl.multiple_of(second * ROWS, ROWS), ROWS), :]
+    blank = jnp.zeros((ROWS, WIDTH), BF16)
+
+    def ids_of(number):
+        at = jnp.maximum(number, 0) * 2
+        ids = [jnp.where(number < 0, -1, pairs_ref[at + i]) for i in range(2)]
+        return ids, [base[pl.ds(pl.multiple_of(jnp.maximum(i, 0) * ROWS, ROWS), ROWS), :] for i in ids]
+
+    def weights(number):
+        _, (tile_a, tile_b) = ids_of(number)
         high_a, low_a = high_low(tile_a)
         left = jnp.concatenate([high_a, high_a, low_a, low_a], axis=0)
         last = tile_b[8:]
@@ -183,40 +206,64 @@
             preferred_element_type=F32,
         )
         root = lax.rsqrt(forms[:, WIDTH:])
-        weight = forms[:, :WIDTH] * root * (root * root)
-        high, low = high_low(weight)
-
-        def places(tile):
-            value = jnp.concatenate(high_low(tile[8:]), axis=0)
-            return jnp.concatenate([value, value], axis=1)
-
+        return high_low(forms[:, :WIDTH] * root * (root * root))
+
+    def places(tile):
+        return jnp.concatenate(high_low(tile[8:]), axis=0)
+
+    def two_pairs(number, matrix):
+        ids, tiles = zip(*[ids_of(number + i) for i in range(2)])
+        value = matrix[...]
+        first = [places(tile[0]) for tile in tiles]
+        second = [places(tile[1]) for tile in tiles]
         on_b = jnp.dot(
-            places(tile_a), jnp.concatenate([high, low], axis=0), preferred_element_type=F32
+            jnp.concatenate([jnp.concatenate([p, p], axis=1) for p in first], axis=0),
+            value,
+            preferred_element_type=F32,
         )
         on_a = lax.dot_general(
-            places(tile_b),
-            jnp.concatenate([high, low], axis=1),
+            jnp.concatenate(
+                [
+                    jnp.concatenate([second[0], blank], axis=1),
+                    jnp.concatenate([blank, second[1]], axis=1),
+                ],
+                axis=0,
+            ),
+            value,
             (((1,), (1,)), ((), ())),
             preferred_element_type=F32,
         )
-        return [
-            tile[8:] * sums[6:7] - (sums[:8] + sums[8:])
-            for tile, sums in ((tile_a, on_a), (tile_b, on_b))
-        ]
-
-    def step_pairs(step, carry):
+        out = []
+        for i in range(2):
+            sums = on_a[i * ROWS : (i + 1) * ROWS]
+            sums = sums[:, :WIDTH] + sums[:, WIDTH:]
+            for side, got in ((0, sums), (1, on_b[i * ROWS : (i + 1) * ROWS, i * WIDTH : (i + 1) * WIDTH])):
+                force = tiles[i][side][8:] * got[6:7] - (got[:8] + got[8:])
+                out.append((jnp.where(ids[i][side] < 0, slots, ids[i][side]), force))
+        return out
+
+    def half(number, fill, drain):
         done = []
-        for part in range(UNROLL):
-            at = (step * UNROLL + part) * 2
-            ids = [pairs_ref[at], pairs_ref[at + 1]]
-            forces = one_pair(jnp.maximum(ids[0], 0), jnp.maximum(ids[1], 0))
-            done += [(jnp.where(i < 0, slots, i), force) for i, force in zip(ids, forces)]
+        for part in range(UNROLL // 2):
+            for i in range(2):
+                for k, value in enumerate(weights(number + part * 2 + i)):
+                    fill[part][pl.ds(k * WIDTH, WIDTH), pl.ds(i * WIDTH, WIDTH)] = value
+            done += two_pairs(number - UNROLL + part * 2, drain[part])
         for i, force in done:
             place = pl.ds(pl.multiple_of(i * 8, 8), 8)
             total[place, :] = total[place, :] + force
-        return carry
-
-    lax.fori_loop(0, (live_ref[0] + UNROLL - 1) // UNROLL, step_pairs, 0)
+
+    count = UNROLL // 2
+    even, odd = matrices[:count], matrices[count:]
+    for matrix in matrices:
+        matrix[...] = jnp.zeros_like(matrix)
+
+    def step_pairs(step, carry):
+        half(step * 2 * UNROLL, even, odd)
+        half(step * 2 * UNROLL + UNROLL, odd, even)
+        return carry
+
+    lax.fori_loop(0, (live_ref[0] + 3 * UNROLL - 1) // (2 * UNROLL), step_pairs, 0)
 
     def finish(step, carry):
         for k in range(3):
@@ -283,8 +330,7 @@
     zero = jnp.zeros((KC,), F32)
     squares = [zero] * 9 + [-2.0 * c for c in centers] + [one, one, square, zero]
     left = jnp.concatenate([strength, jnp.stack(squares, axis=1)], axis=0)
-    right = [zero] + centers + [zero, zero, one, zero] + [zero] * 8
-    return left, jnp.stack(right, axis=0)
+    return left
 
 
 def on_device(positions, vectors, send_slots, pairs, coarse):
@@ -337,8 +383,8 @@
         "far",
         array(blocks, 3 * WIDTH),
         [VM, VM, VM],
-        [pltpu.VMEM((64, WIDTH), F32)],
-        (base, *far_sides(moments)),
+        [pltpu.VMEM((192, WIDTH), F32)] * FAR_GROUPS,
+        (positions, base, far_sides(moments)),
         cost=pl.CostEstimate(flops=10**9, bytes_accessed=5 * 10**6, transcendentals=4 * 10**6),
     )
     live = jnp.sum((pairs[:, 0] >= 0).astype(jnp.int32)).reshape(1)
@@ -347,8 +393,9 @@
         "near",
         array(slots, 3 * WIDTH),
         [SM, SM, VM],
-        [pltpu.VMEM((slots * ROWS, WIDTH), F32), pltpu.VMEM((slots * 8 + 8, WIDTH), F32)],
-        (live, pairs.reshape(-1), got),
+        [pltpu.VMEM((slots * ROWS, WIDTH), F32), pltpu.VMEM((slots * 8 + 8, WIDTH), F32)]
+        + [pltpu.VMEM((2 * WIDTH, 2 * WIDTH), BF16)] * UNROLL,
+        (live, jnp.pad(pairs, ((0, 3 * UNROLL), (0, 0)), constant_values=-1).reshape(-1), got),
     )
     returned = lax.all_to_all(
         partial_sums.reshape(devices, capacity, 3 * WIDTH),

time: 179 us -> 106 us (0.59)
  Pallas kernels: 128 us -> 78.4 us
  starting transfers between devices: 39.4 us -> 15.5 us
    pallas_call x5, Pallas kernels: 128 us -> 78.4 us  [call(): pl.pallas_call(kernel, name=name, out_shape=outs, in_specs=in_specs, out_...]
    all_to_all x1, starting transfers between devices: 27.9 us -> 4.01 us  [on_device(): lax.all_to_all(partial_sums.reshape(devices, capacity, 3 * WIDTH), axes,...]
  transfers between devices with their start and end apart: 2 -> 2, of which waited for: 0 -> 0; matrix products, arithmetic and copies ran while one was open for 4% -> 6% of each run, Pallas kernels for 48% -> 47%
where the time goes in v2:
time: 106 us; the launch traced here: 105 us
  Pallas kernels  78.4 us (74%)
  starting transfers between devices  15.5 us (15%)
  local copies, waits for them, and re-layouts  5.92 us (6%)
  other arithmetic  4.79 us (5%)
    pallas_call x5, Pallas kernels, call(): pl.pallas_call(kernel, name=name, out_shape=outs, in_specs=in_specs, out_...  78.4 us
    all_to_all x1, starting transfers between devices, on_device(): lax.all_to_all(send.reshape(devices, capacity * 8, WIDTH), axes, split_ax...  11.5 us
    all_to_all x1, starting transfers between devices, on_device(): lax.all_to_all(partial_sums.reshape(devices, capacity, 3 * WIDTH), axes,...  4.01 us
    unnamed x12, local copies, waits for them, and re-layouts  3.47 us
  transfers between devices with their start and end apart: 2, of which 0 were waited for; matrix products, arithmetic and copies ran while one was open for 6% of the time, Pallas kernels for 47%

profile of v2, /device:TPU:1, one launch (start us, length us, event | category | flops | bytes accessed | tf_op | source)
XLA Modules:
  0.0 105.1 jit_solution(3227122971691656566)
XLA Ops:
  0.0 0.8 copy.42
  0.8 0.1 reshape.368.ids_ref
  0.9 0.0 copy-start
  0.9 1.4 %copy-done = f32[512,768]{1,0:T(8,128)S(1)} copy-done((f32[512,768]{1,0:T(8,128)S(1)}, f32[512,768]{1,0:T(8,128)}, u32[]{:S(2)}) %copy-start) | copy-done | bytes 1572888
  2.3 0.0 copy-start.1
  2.3 1.1 %copy-done.1 = f32[512,384]{1,0:T(8,128)S(1)} copy-done((f32[512,384]{1,0:T(8,128)S(1)}, f32[512,384]{1,0:T(8,128)}, u32[]{:S(2)}) %copy-start.1) | copy-done | bytes 786456
  3.4 6.8 %pack.1 = (f32[4096,128]{1,0:T(8,128)}, f32[8192,128]{1,0:T(8,128)}) custom-call(s32[512]{0:T(512)S(1)} %reshape.368.ids_ref, f32[512,384]{1,0:T(8,128)S(1)} %copy-done.1, f32[512,768]{1,0:T(8,128)S(1)} %copy-done), custom_call_target="tpu_custom_call" | custom-call | tf_op jit(solution)/shard_map/pack/pallas_call | solution.py:302
  10.2 0.0 copy-start.4
  10.2 0.0 copy-start.3
  10.2 11.5 %all-to-all-start = ((f32[128,32,128]{2,1,0:T(8,128)}), f32[128,32,128]{2,1,0:T(8,128)S(1)}, u32[]{:S(2)}, u32[]{:S(2)}) async-start(f32[128,32,128]{2,1,0:T(8,128)} %bitcast.27), calls=%async_computation | async-start | bytes 4194304 | tf_op jit(solution)/shard_map/all_to_all | solution.py:353
  21.7 2.1 %multiply_reduce_fusion = (f32[512]{0:T(512)S(1)}, f32[512]{0:T(512)S(1)}, f32[512]{0:T(512)S(1)}, f32[512]{0:T(512)S(1)}, f32[512]{0:T(512)S(1)}, /*index=5*/f3...) fusion(f32[512,768]{1,0:T(8,128)} %vec_ref.1), kind=kLoop, calls=%fused_computation | loop fusion | flops 1175040 | bytes 1591296 | tf_op jit(solution)/shard_map/reduce_sum | solution.py:359
  23.8 0.1 stack.64
  23.8 0.0 copy-done.4
  23.8 0.4 fusion.1
  24.2 0.1 reshape.373
  24.4 31.3 %moments.1 = f32[8,128]{1,0:T(8,128)S(1)} custom-call(f32[8,128]{1,0:T(8,128)S(1)} %pad_bitcast_fusion.refs_0_), custom_call_target="tpu_custom_call" | custom-call | tf_op jit(solution)/shard_map/moments/pallas_call | solution.py:302
  55.7 0.0 copy-done.3
  55.7 0.1 copy.48
  55.9 0.1 reshape.367.pairs_ref
  56.0 0.6 fusion.7
  56.7 0.0 all-to-all-done
  56.7 20.1 %near.1 = f32[512,384]{1,0:T(8,128)S(1)} custom-call(s32[1]{0:T(128)} %bitcast.live_ref, s32[536]{0:T(1024)S(1)} %reshape.367.pairs_ref, f32[4096,128]{1,0:T(8,128)S(1)} %bitcast.25), custom_call_target="tpu_custom_call" | custom-call | tf_op jit(solution)/shard_map/near/pallas_call | solution.py:302
  76.8 0.0 copy-start.2
  76.8 1.1 %reshape.371 = f32[128,4,384]{2,1,0:T(4,128)} reshape(f32[512,384]{1,0:T(8,128)S(1)} %near.1) | data formatting | bytes 1572864 | tf_op jit(solution)/shard_map/reshape | solution.py:401
  77.9 4.0 %all-to-all-start.1 = ((f32[128,4,384]{2,1,0:T(4,128)}), f32[128,4,384]{2,1,0:T(4,128)S(1)}, u32[]{:S(2)}, u32[]{:S(2)}) async-start(f32[128,4,384]{2,1,0:T(4,128)} %reshape.371), calls=%async_computation.1 | async-start | bytes 1572864 | tf_op jit(solution)/shard_map/all_to_all | solution.py:400
  81.9 0.1 reshape_reshape.3.ids_ref
  82.1 0.3 div.79
  82.4 0.1 stack.68
  82.5 2.0 %multiply_reduce_fusion.9 = (f32[64]{0:T(128)S(1)}, f32[64]{0:T(128)S(1)}, f32[64]{0:T(128)S(1)}, f32[64]{0:T(128)S(1)}, f32[64]{0:T(128)S(1)}, /*index=5*/f32[6...) fusion(f32[64,3,3]{2,1,0:T(4,128)S(1)} %div.79), kind=kLoop, calls=%fused_computation.16 | loop fusion | flops 960 | bytes 4608 | tf_op jit(solution)/shard_map/div | solution.py:324
  84.5 0.1 select_maximum_fusion
  84.6 0.1 copy.46.left_ref
  84.7 0.0 copy-done.2
  84.7 17.9 %far.1.far_ref = f32[512,384]{1,0:T(8,128)S(1)} custom-call(f32[512,384]{1,0:T(8,128)S(1)} %copy-done.2, f32[8192,128]{1,0:T(8,128)} %get-tuple-element.8.base_ref, f32[128,16]{1,0:T(8,128)S(1)} %copy.46.left_ref), custom_call_target="tpu_custom_call" | custom-call | flops 1000000000 | bytes 5000000 | tf_op jit(solution)/shard_map/far/pallas_call | solution.py:302
  102.6 0.0 all-to-all-done.1
  102.6 0.3 reshape.372.got_ref
  102.9 2.2 %final.1 = f32[512,384]{1,0:T(8,128)} custom-call(s32[1,512]{1,0:T(1,128)S(1)} %reshape_reshape.3.ids_ref, f32[512,384]{1,0:T(8,128)S(1)} %reshape.372.got_ref, f32[512,384]{1,0:T(8,128)S(1)} %far.1.far_ref), custom_call_target="tpu_custom_call" | custom-call | tf_op jit(solution)/shard_map/final/pallas_call | solution.py:302
  (10 shorter events, 0.1 us)
Async XLA Ops:
  0.9 1.4 %copy-start = (f32[512,768]{1,0:T(8,128)S(1)}, f32[512,768]{1,0:T(8,128)}, u32[]{:S(2)}) copy-start(f32[512,768]{1,0:T(8,128)} %vec_ref.1) | copy-start | bytes 4718596
  2.3 1.1 %copy-start.1 = (f32[512,384]{1,0:T(8,128)S(1)}, f32[512,384]{1,0:T(8,128)}, u32[]{:S(2)}) copy-start(f32[512,384]{1,0:T(8,128)} %pos_ref.3) | copy-start | bytes 2359300
  10.2 13.6 %copy-start.4 = (s32[512]{0:T(512)S(1)}, s32[512]{0:T(512)}, u32[]{:S(2)}) copy-start(s32[512]{0:T(512)} %param.9) | copy-start | bytes 6148
  10.2 45.5 %copy-start.3 = (s32[256,2]{0,1:T(2,128)S(1)}, s32[256,2]{0,1:T(2,128)}, u32[]{:S(2)}) copy-start(s32[256,2]{0,1:T(2,128)} %param.8) | copy-start | bytes 6148
  10.2 46.5 %all-to-all-start = ((f32[128,32,128]{2,1,0:T(8,128)}), f32[128,32,128]{2,1,0:T(8,128)S(1)}, u32[]{:S(2)}, u32[]{:S(2)}) async-start(f32[128,32,128]{2,1,0:T(8,128)} %bitcast.27), calls=%async_computation | async-start | bytes 4194304 | tf_op jit(solution)/shard_map/all_to_all | solution.py:353
  76.8 7.9 %copy-start.2 = (f32[512,384]{1,0:T(8,128)S(1)}, f32[512,384]{1,0:T(8,128)}, u32[]{:S(2)}) copy-start(f32[512,384]{1,0:T(8,128)} %pos_ref.3) | copy-start | bytes 2359300
  77.9 24.7 %all-to-all-start.1 = ((f32[128,4,384]{2,1,0:T(4,128)}), f32[128,4,384]{2,1,0:T(4,128)S(1)}, u32[]{:S(2)}, u32[]{:S(2)}) async-start(f32[128,4,384]{2,1,0:T(4,128)} %reshape.371), calls=%async_computation.1 | async-start | bytes 1572864 | tf_op jit(solution)/shard_map/all_to_all | solution.py:400

commit v3 on v0

v3 whole, which is shorter than its diff:
```python
import math

import jax
import jax.numpy as jnp
from jax import lax
from jax.experimental import pallas as pl
from jax.experimental.pallas import tpu as pltpu
from jax.sharding import PartitionSpec as P

MESH = pl.DeviceIdType.MESH
F32 = jnp.float32
BF16 = jnp.bfloat16
KC = 64
WIDTH = 128
MIDDLE = 2.0
ROWS = 16
UNROLL = 2
CUBE_UNROLL = 4
CAP = 4
BACK = 12
FAR_GROUPS = 2
LOADS = 8
SIDE_X = 4
VMEM_LIMIT = 60 * 2**20


def high_low(value):
    high = value.astype(BF16)
    return high, (value - high.astype(F32)).astype(BF16)


def couplings(tensor):
    scale = WIDTH**-0.25
    rows = [scale * math.sqrt(1.5) * tensor[k][k] for k in range(3)]
    for k, l in ((0, 1), (0, 2), (1, 2)):
        rows.append(scale * math.sqrt(0.75) * (tensor[k][l] + tensor[l][k]))
        rows.append(scale * 0.5 * (tensor[k][l] - tensor[l][k]))
    return rows


def features(place, tensor):
    square = place[0] * place[0] + place[1] * place[1] + place[2] * place[2] + 0.125
    upper = square.astype(BF16).astype(F32)
    one = jnp.ones_like(square)
    return couplings(tensor) + list(place) + [upper, square - upper, one, one]


def other(step):
    gx, yz = lax.axis_index("gx"), lax.axis_index("yz")
    size_yz = lax.axis_size("yz")
    chips = lax.axis_size("gx") * size_yz // 2
    side_x, side_z = SIDE_X, size_yz // 2
    side_y = lax.axis_size("gx") // side_x
    chip, core = lax.rem(step, chips), step // chips
    first = lax.rem(chip, side_y)
    second = first + lax.rem(chip // side_y, side_x)
    third = second + chip // (side_y * side_x)
    y = lax.rem(gx // side_x + first, side_y)
    x = lax.rem(lax.rem(gx, side_x) + second, side_x)
    z = lax.rem(yz // 2 + third, side_z)
    return y * side_x + x, z * 2 + lax.rem(lax.rem(yz, 2) + core, 2)


def pack_group(step, pos_ref, vec_ref, base_ref, table, packed):
    rows = pl.ds(pl.multiple_of(step * 8, 8), 8)
    place = [pos_ref[rows, pl.ds(k * WIDTH, WIDTH)] - MIDDLE for k in range(3)]
    line = [vec_ref[rows, pl.ds(k * WIDTH, WIDTH)] for k in range(3)]
    burg = [vec_ref[rows, pl.ds((3 + k) * WIDTH, WIDTH)] for k in range(3)]
    for row, value in enumerate(features(place, [[b * l for l in line] for b in burg])):
        base_ref[pl.ds(step * 8 * ROWS + row, 8, stride=ROWS), :] = value
        if row < 9:
            table[rows, pl.ds(row * WIDTH, WIDTH)] = value
    square = line[0] * line[0] + line[1] * line[1] + line[2] * line[2]
    inverse = lax.rsqrt(jnp.maximum(square, 1e-36))
    side = jnp.where(line[2] < 0, -inverse, inverse)
    length = square * side
    tilt = 1.0 / (1.0 + line[2] * side)
    out = place + [b * length for b in burg] + [line[0] * side * tilt, line[1] * side * tilt]
    for row, value in enumerate(out):
        packed[pl.ds(step * 64 + row, 8, stride=8), :] = value


def cell_sums(coarse_ref, table):
    blocks = table.shape[0]
    cells = lax.broadcasted_iota(jnp.int32, (KC, blocks), 0)
    chosen = jnp.where(cells == coarse_ref[...], 1.0, 0.0).astype(BF16)
    parts = []
    for m in range(9):
        high, low = high_low(table[:, m * WIDTH : (m + 1) * WIDTH])
        parts.append(
            jnp.dot(chosen, high, preferred_element_type=F32)
            + jnp.dot(chosen, low, preferred_element_type=F32)
        )
    high, low = high_low(jnp.concatenate(parts, axis=1))
    row = lax.broadcasted_iota(jnp.int32, (ROWS, 9 * WIDTH), 0)
    lane = lax.broadcasted_iota(jnp.int32, (ROWS, 9 * WIDTH), 1)
    along = jnp.where((lane >= row * WIDTH) & (lane < row * WIDTH + WIDTH), 1.0, 0.0).astype(BF16)
    sums = [
        lax.dot_general(along, value, (((1,), (1,)), ((), ())), preferred_element_type=F32)
        for value in (high, low)
    ]
    sums = sums[0] + sums[1]
    return jnp.concatenate([sums[:8], sums[8:]], axis=1)


def far_left(sums, norm):
    row = lax.broadcasted_iota(jnp.int32, (ROWS, KC), 0)
    cell = lax.broadcasted_iota(jnp.int32, (ROWS, KC), 1)
    turned = (row == 4) | (row == 6) | (row == 8)
    square = WIDTH**-0.5
    strength = sums * jnp.where(turned, 2.0 / square * norm, norm / (1.5 * square))
    centers = [(c + (0.5 - MIDDLE)).astype(F32) for c in (cell // 16, cell // 4 % 4, cell % 4)]
    whole = centers[0] * centers[0] + centers[1] * centers[1] + centers[2] * centers[2]
    squares = jnp.where((row == 12) | (row == 13), 1.0, 0.0)
    squares = jnp.where(row == 14, whole + (1.0 - 0.125), squares)
    for k in range(3):
        squares = jnp.where(row == 9 + k, -2.0 * centers[k], squares)
    left = jnp.transpose(jnp.concatenate([strength, squares], axis=1))
    high, low = high_low(left)
    return jnp.concatenate([high, high, low], axis=1)


def stacked(tile):
    return jnp.concatenate(high_low(tile), axis=0)


def beside(first, second):
    blank = jnp.zeros_like(first)
    return jnp.concatenate(
        [jnp.concatenate([first, blank], axis=1), jnp.concatenate([blank, second], axis=1)], axis=0
    )


def forms_of(lefts, rights):
    return lax.dot_general(
        jnp.concatenate(lefts, axis=0),
        beside(*rights),
        (((0,), (0,)), ((), ())),
        preferred_element_type=F32,
    )


def whole_kernel(
    ids_ref,
    pairs_ref,
    id_rows,
    pair_rows,
    coarse_ref,
    pos_hbm,
    vec_hbm,
    o_ref,
    pos_ref,
    vec_ref,
    packed,
    send_ref,
    got_ref,
    base_ref,
    table,
    place_base,
    form_base,
    cubes,
    forces,
    out_ref,
    back_ref,
    mine,
    near,
    total,
    far,
    load_sem,
    send_sem,
    recv_sem,
    bulk_sem,
    round_sem,
    *buffers,
):
    packed_rows, place_rows_ref, form_rows_ref = [
        ref.reshape(ref.shape[0] * ref.shape[1], WIDTH) for ref in (packed, place_base, form_base)
    ]
    tiles, matrices = buffers[:FAR_GROUPS], buffers[FAR_GROUPS:]
    gx, yz = lax.axis_index("gx"), lax.axis_index("yz")
    size_gx, size_yz = lax.axis_size("gx"), lax.axis_size("yz")
    devices = size_gx * size_yz
    me = gx * size_yz + yz
    blocks = pos_ref.shape[0]
    count = pairs_ref.shape[1]
    loaded = blocks // LOADS

    def along_yz(step):
        return gx, lax.rem(yz + step, size_yz)

    def along_gx(step):
        return lax.rem(gx + step, size_gx), yz

    def loads(step):
        rows = pl.ds(pl.multiple_of(step * loaded, loaded), loaded)
        return [
            pltpu.make_async_copy(source.at[rows], target.at[rows], load_sem.at[k, step])
            for k, (source, target) in enumerate(((pos_hbm, pos_ref), (vec_hbm, vec_ref)))
        ]

    barrier = pltpu.get_barrier_semaphore()
    for turn, size in ((along_yz, size_yz), (along_gx, size_gx)):
        for step in range(1, size):
            pl.semaphore_signal(barrier, inc=1, device_id=turn(step), device_id_type=MESH)
    for step in range(LOADS):
        for copy in loads(step):
            copy.start()

    def pack(step, carry):
        for copy in loads(step):
            copy.wait()

        def group(inner, carry):
            pack_group(step * (loaded // 8) + inner, pos_ref, vec_ref, base_ref, table, packed_rows)
            return carry

        return lax.fori_loop(0, loaded // 8, group, carry)

    lax.fori_loop(0, LOADS, pack, 0)
    pl.semaphore_wait(barrier, size_yz + size_gx - 2)
    for step in range(1, size_yz):
        pl.semaphore_signal(round_sem, inc=1, device_id=along_yz(step), device_id_type=MESH)

    def exchange(source, held, turn, size, sem):
        return [
            pltpu.make_async_remote_copy(
                src_ref=source,
                dst_ref=held.at[step],
                send_sem=send_sem.at[sem + step],
                recv_sem=recv_sem.at[sem + step],
                device_id=turn(step),
                device_id_type=MESH,
            )
            for step in range(1, size)
        ]

    def gathered(source, held, copies):
        for copy in copies:
            copy.wait()
        result = source[...]
        for step in range(1, len(copies) + 1):
            result = result + held[step]
        return result

    mine[...] = cell_sums(coarse_ref, table)
    over_yz = exchange(mine, near, along_yz, size_yz, 0)
    over_gx = exchange(total, far, along_gx, size_gx, size_yz)
    for copy in over_yz:
        copy.start()
    pl.semaphore_wait(round_sem, size_yz - 1)

    chunk = CAP * 8
    half = chunk // 2

    def pick(device):
        for slot in range(CAP):
            source = jnp.maximum(ids_ref[slot, device], 0)
            send_ref[pl.ds(device * chunk + slot, 8, stride=CAP), :] = packed[
                source
            ]

    def bulk(step, source, target, pitch, at, size, sem):
        to_gx, to_yz = other(step)
        device = to_gx * size_yz + to_yz
        return pltpu.make_async_remote_copy(
            src_ref=source.at[pl.ds(pl.multiple_of(device * pitch + at, 8), size)],
            dst_ref=target.at[pl.ds(pl.multiple_of(me * pitch + at, 8), size)],
            send_sem=bulk_sem.at[sem],
            recv_sem=bulk_sem.at[sem + 1],
            device_id=(to_gx, to_yz),
            device_id_type=MESH,
        )

    def all_of(source, target, size, sem):
        rows = pl.ds(0, (devices - 1) * size)
        return pltpu.make_async_remote_copy(
            src_ref=source.at[rows],
            dst_ref=target.at[rows],
            send_sem=bulk_sem.at[sem],
            recv_sem=bulk_sem.at[sem + 1],
            device_id=other(1),
            device_id_type=MESH,
        )

    def send_first(step, carry):
        to_gx, to_yz = other(step)
        pick(to_gx * size_yz + to_yz)
        bulk(step, send_ref, got_ref, chunk, 0, half, 0).start()
        return carry

    def send_second(step, carry):
        bulk(step, send_ref, got_ref, chunk, half, half, 2).start()
        return carry

    lax.fori_loop(1, 1 + devices // 4, send_first, 0)
    total[...] = gathered(mine, near, over_yz)
    for copy in over_gx:
        copy.start()
    lax.fori_loop(1 + devices // 4, devices, send_first, 0)
    lax.fori_loop(1, devices, send_second, 0)
    pick(me)
    rows = pl.ds(pl.multiple_of(me * chunk, chunk), chunk)
    got_ref[rows, :] = send_ref[rows, :]
    for matrix in matrices:
        matrix[...] = jnp.zeros_like(matrix)
    form_base[...] = jnp.zeros_like(form_base)

    sums = gathered(total, far, over_gx)
    left = far_left(
        jnp.concatenate([sums[:, :KC], sums[:, KC:]], axis=0),
        1.0 / (math.sqrt(blocks * devices * WIDTH / KC) * math.sqrt(KC)),
    )

    def far_step(step, carry):
        for part in range(FAR_GROUPS):
            far_group(step * FAR_GROUPS + part, left, pos_ref, base_ref, o_ref, tiles[part])
        return carry

    lax.fori_loop(0, blocks // (8 * FAR_GROUPS), far_step, 0)

    def came(step, slot, first, last):
        return [
            got_ref[pl.ds(step * 8 * chunk + CAP * k + slot, 8, stride=chunk), :]
            for k in range(first, last)
        ]

    all_of(send_ref, got_ref, half, 0).wait_recv()

    def place_rows(step, carry):
        for slot in range(CAP):
            place = came(step, slot, 0, 3)
            square = place[0] * place[0] + place[1] * place[1] + place[2] * place[2] + 0.125
            upper = square.astype(BF16).astype(F32)
            one = jnp.ones_like(square)
            values = place + [upper, square - upper, one, one, jnp.zeros_like(square)]
            for row, value in enumerate(values):
                place_rows_ref[pl.ds(step * 64 * CAP + slot * 8 + row, 8, stride=8 * CAP), :] = value
        return carry

    lax.fori_loop(0, devices // 8, place_rows, 0)
    row = lax.broadcasted_iota(jnp.int32, (8, WIDTH), 0)

    def tile_of(base, side, number):
        return base[jnp.maximum(pairs_ref[side, number], 0)]

    def cube_step(step, carry):
        for part in range(CUBE_UNROLL):
            number = (step * CUBE_UNROLL + part) * 2
            lefts, rights = [], []
            for i in range(2):
                value = stacked(tile_of(place_base, 0, number + i))
                lefts += [value, value]
                last = tile_of(place_base, 1, number + i)
                turned = pltpu.roll(last, 2, 0)
                last = jnp.where(
                    row < 3, -2.0 * last, jnp.where(row < 5, 1.0, jnp.where(row < 7, turned, 0.0))
                )
                high, low = high_low(last)
                rights.append(jnp.concatenate([high, high, low, low], axis=0))
            root = lax.rsqrt(forms_of(lefts, rights))
            rows = pl.ds(pl.multiple_of(number * (WIDTH // 2), WIDTH), WIDTH)
            cubes[rows, :] = root * (root * root)
        return carry

    lax.fori_loop(0, count // (2 * CUBE_UNROLL), cube_step, 0)
    all_of(send_ref, got_ref, half, 2).wait_recv()

    def form_rows(step, carry):
        for slot in range(CAP):
            got = came(step, slot, 3, 8)
            square = got[3] * got[3] + got[4] * got[4]
            inverse = 1.0 / (1.0 + square)
            line = [2.0 * got[3] * inverse, 2.0 * got[4] * inverse, (1.0 - square) * inverse]
            for row, value in enumerate(couplings([[b * l for l in line] for b in got[:3]])):
                form_rows_ref[
                    pl.ds(step * 8 * ROWS * CAP + slot * ROWS + row, 8, stride=ROWS * CAP), :
                ] = value
        return carry

    lax.fori_loop(0, devices // 8, form_rows, 0)

    def fill(number, matrix):
        lefts, rights = [], []
        for i in range(2):
            high, low = high_low(tile_of(form_base, 0, number + i))
            lefts += [high, high, low]
            high, low = high_low(tile_of(form_base, 1, number + i))
            rights.append(jnp.concatenate([high, low, high], axis=0))
        rows = pl.ds(pl.multiple_of(number * (WIDTH // 2), WIDTH), WIDTH)
        high, low = high_low(forms_of(lefts, rights) * cubes[rows, :])
        matrix[pl.ds(0, WIDTH), :] = high
        matrix[pl.ds(WIDTH, WIDTH), :] = low

    def drain(number, at, matrix):
        value = matrix[...]
        places = [[tile_of(place_base, side, number + i) for i in range(2)] for side in range(2)]
        first, second = [[stacked(tile) for tile in side] for side in places]
        on_b = jnp.dot(
            jnp.concatenate([jnp.concatenate([p, p], axis=1) for p in first], axis=0),
            value,
            preferred_element_type=F32,
        )
        on_a = lax.dot_general(
            beside(*second), value, (((1,), (1,)), ((), ())), preferred_element_type=F32
        )
        for i in range(2):
            on_first = on_a[i * ROWS : (i + 1) * ROWS]
            on_first = on_first[:, :WIDTH] + on_first[:, WIDTH:]
            on_second = on_b[i * ROWS : (i + 1) * ROWS, i * WIDTH : (i + 1) * WIDTH]
            for side, got in enumerate((on_first, on_second)):
                force = places[side][i] * got[5:6] - (got[:8] + got[8:])
                forces[side, pl.ds(pl.multiple_of((at + i) * 8, 8), 8), :] = force

    even, odd = matrices[:UNROLL], matrices[UNROLL:]

    def half_step(number, filled, drained):
        for part in range(UNROLL):
            fill(jnp.minimum(number + 2 * part, count - 2), filled[part])
            at = number + 2 * part
            before = jnp.clip(at - 2 * UNROLL, 0, count - 2)
            drain(before, at, drained[part])

    def pair_step(step, carry):
        half_step(step * 4 * UNROLL, even, odd)
        half_step(step * 4 * UNROLL + 2 * UNROLL, odd, even)
        return carry

    lax.fori_loop(0, pl.cdiv(count + 2 * UNROLL, 4 * UNROLL), pair_step, 0)
    parts = []
    for side in range(2):
        parts.append(
            jnp.concatenate(
                [
                    forces[side, pl.ds(16 * UNROLL + k, count, stride=8), :]
                    for k in range(3)
                ],
                axis=1,
            )
        )
    high, low = high_low(jnp.concatenate(parts, axis=0))
    ids = jnp.concatenate([pair_rows[pl.ds(0, 1), :], pair_rows[pl.ds(1, 1), :]], axis=1)
    slots = lax.broadcasted_iota(jnp.int32, (devices, 2 * count), 0) * CAP
    for slot in range(CAP):
        chosen = jnp.where(slots + slot == ids, 1.0, 0.0).astype(BF16)
        value = jnp.dot(chosen, high, preferred_element_type=F32) + jnp.dot(
            chosen, low, preferred_element_type=F32
        )
        for k in range(3):
            out_ref[pl.ds(CAP * k + slot, devices, stride=ROWS), :] = value[
                :, k * WIDTH : (k + 1) * WIDTH
            ]

    def send_back(step, carry):
        bulk(step, out_ref, back_ref, ROWS, 0, BACK, 4).start()
        return carry

    lax.fori_loop(1, devices, send_back, 0)
    rows = pl.ds(pl.multiple_of(me * ROWS, ROWS), ROWS)
    back_ref[rows, :] = out_ref[rows, :]
    all_of(send_ref, got_ref, half, 0).wait_send()
    all_of(send_ref, got_ref, half, 2).wait_send()
    done = all_of(out_ref, back_ref, BACK, 4)
    done.wait_send()
    done.wait_recv()

    back = jnp.concatenate(
        [
            jnp.concatenate(
                [back_ref[pl.ds(CAP * k + slot, devices, stride=ROWS), :] for k in range(3)], axis=1
            )
            for slot in range(CAP)
        ],
        axis=0,
    )
    high, low = high_low(back)
    ids = jnp.concatenate([id_rows[pl.ds(slot, 1), :] for slot in range(CAP)], axis=1)
    for step in range(blocks // WIDTH):
        index = lax.broadcasted_iota(jnp.int32, (WIDTH, devices * CAP), 0) + step * WIDTH
        chosen = jnp.where(index == ids, 1.0, 0.0).astype(BF16)
        rows = pl.ds(step * WIDTH, WIDTH)
        o_ref[rows, :] = (
            o_ref[rows, :]
            + jnp.dot(chosen, high, preferred_element_type=F32)
            + jnp.dot(chosen, low, preferred_element_type=F32)
        )


def far_group(step, left, pos_ref, base_ref, o_ref, tile):
    for part in range(4):
        at = (step * 8 + part * 2) * ROWS
        both = jnp.concatenate(
            [base_ref[pl.ds(pl.multiple_of(at + i * ROWS, ROWS), ROWS), :] for i in range(2)], axis=1
        )
        high, low = high_low(both)
        forms = jnp.dot(
            left, jnp.concatenate([high, low, high], axis=0), preferred_element_type=F32
        )
        root = lax.rsqrt(forms[KC:])
        weight = forms[:KC] * root * (root * root)
        w = [weight[8 * v : 8 * v + 8] for v in range(8)]
        s = [w[2 * i] + w[2 * i + 1] for i in range(4)]
        sums = [
            1.5 * (s[3] - s[0]) + 0.5 * (s[2] - s[1]),
            (w[1] + w[3]) + (w[5] + w[7]),
            (s[0] + s[1]) + (s[2] + s[3]),
        ]
        for q, value in enumerate(sums):
            for i in range(2):
                tile[pl.ds(q * 64 + (part * 2 + i) * 8, 8), :] = value[:, i * WIDTH : (i + 1) * WIDTH]
    along_x, upper, t = (
        [tile[pl.ds(q * 64 + r, 8, stride=8), :] for r in range(8)] for q in range(3)
    )
    first = (t[0] + t[1]) + (t[2] + t[3])
    second = (t[4] + t[5]) + (t[6] + t[7])
    whole = first + second
    m = [t[i] + t[i + 4] for i in range(4)]
    centers = [
        sum(along_x[1:], along_x[0]),
        2.0 * sum(upper[1:], upper[0]) - 1.5 * first - 0.5 * second,
        1.5 * (m[3] - m[0]) + 0.5 * (m[2] - m[1]),
    ]
    rows = pl.ds(pl.multiple_of(step * 8, 8), 8)
    for k in range(3):
        column = pl.ds(k * WIDTH, WIDTH)
        o_ref[rows, column] = (pos_ref[rows, column] - MIDDLE) * whole - centers[k]


VM = pl.BlockSpec(memory_space=pltpu.VMEM)
SM = pl.BlockSpec(memory_space=pltpu.SMEM)
ANY = pl.BlockSpec(memory_space=pl.ANY)


def on_device(positions, vectors, send_slots, pairs, coarse):
    size_gx, size_yz = lax.axis_size("gx"), lax.axis_size("yz")
    devices = size_gx * size_yz
    blocks, slots, count = positions.shape[0], devices * CAP, pairs.shape[0]
    ids, pair_ids = send_slots[0].T, pairs.T

    def rows(number, width=WIDTH):
        return pltpu.VMEM((number, width), F32)

    dma = pltpu.SemaphoreType.DMA
    return pl.pallas_call(
        whole_kernel,
        name="forces",
        out_shape=jax.ShapeDtypeStruct((blocks, 3 * WIDTH), F32),
        in_specs=[SM, SM, VM, VM, VM, ANY, ANY],
        out_specs=VM,
        scratch_shapes=[
            rows(blocks, 3 * WIDTH),
            rows(blocks, 6 * WIDTH),
            pltpu.VMEM((blocks, 8, WIDTH), F32),
            rows(slots * 8),
            rows(slots * 8),
            rows(blocks * ROWS),
            rows(blocks, 9 * WIDTH),
            pltpu.VMEM((slots, 8, WIDTH), F32),
            pltpu.VMEM((slots, ROWS, WIDTH), F32),
            rows(count * WIDTH // 2, 2 * WIDTH),
            pltpu.VMEM((2, (count + 6 * UNROLL) * 8, WIDTH), F32),
            rows(devices * ROWS),
            rows(devices * ROWS),
            rows(8),
            pltpu.VMEM((size_yz, 8, WIDTH), F32),
            rows(8),
            pltpu.VMEM((size_gx, 8, WIDTH), F32),
            dma((2, LOADS)),
            dma((size_yz + size_gx,)),
            dma((size_yz + size_gx,)),
            dma((6,)),
            pltpu.SemaphoreType.REGULAR,
        ]
        + [rows(192)] * FAR_GROUPS
        + [pltpu.VMEM((2 * WIDTH, 2 * WIDTH), BF16)] * (2 * UNROLL),
        compiler_params=pltpu.CompilerParams(
            vmem_limit_bytes=VMEM_LIMIT, collective_id=0, has_side_effects=True
        ),
    )(ids, pair_ids, ids, pair_ids, coarse.reshape(1, blocks), positions, vectors)


def solution(mesh):
    placed = (
        P(("gx", "yz"), None),
        P(("gx", "yz"), None),
        P(("gx", "yz"), None, None),
        P(("gx", "yz"), None),
        P(("gx", "yz")),
    )
    return jax.shard_map(
        on_device, mesh=mesh, in_specs=placed, out_specs=P(("gx", "yz"), None), check_vma=False
    )
```

time: 425 us -> 79.5 us (0.19)
  other arithmetic: 209 us -> 0 us
  local copies, waits for them, and re-layouts: 101 us -> 2.06 us
  Pallas kernels: 0 us -> 77.3 us
  blocking collectives: 74.9 us -> 0 us
  starting transfers between devices: 23.6 us -> 0 us
  waiting for transfers between devices: 10.2 us -> 0 us
    reduce_sum x65 -> x0, other arithmetic: 170 us -> none  [the longest x48 97.1 us: far_tile(): jnp.sum(weight * offsets[index], axis=1)]
    gather x68 -> x0, local copies, waits for them, and re-layouts: 81.2 us -> none  [the longest x16 27.5 us: pair_block(): recv_pos[ids_group[:, 1]]]
    pallas_call x0 -> x1, Pallas kernels: none -> 77.3 us  [on_device(): pl.pallas_call(whole_kernel, name='forces', out_shape=jax.ShapeDtypeStruc...]
    psum x1 -> x0, blocking collectives: 74.9 us -> none  [on_device(): total_moments = lax.psum(local_moments, ('gx', 'yz'))]
    all_to_all x3 -> x0, starting transfers between devices: 23.6 us -> none  [the longest x1 11.9 us: on_device(): lax.all_to_all(out_pos, ('gx', 'yz'), split_axis=0, concat_axis=0, tiled=...]
    dynamic_update_slice x32 -> x0, other arithmetic: 21.3 us -> none  [the longest x16 11.2 us: on_device(): lax.map(pair_block, (pair_ids.reshape(-1, group_size, 2), usable.reshape(...]
    squeeze x32 -> x0, local copies, waits for them, and re-layouts: 13 us -> none  [on_device(): lax.map(lambda packed: far_tile(packed[0], packed[1], moments, width), (p...]
    scatter-add x3 -> x0, other arithmetic: 11.9 us -> none  [the longest x1 5.69 us: on_device(): jax.ops.segment_sum(returned, slot_ids.reshape(-1), num_segments=blocks_h...]
  transfers between devices with their start and end apart: 3 -> 0, of which waited for: 1 -> 0; matrix products, arithmetic and copies ran while one was open for 31% -> 0% of each run, Pallas kernels for 0% -> 0%
where the time goes in v3:
time: 79.5 us; the launch traced here: 79.3 us
  Pallas kernels  77.3 us (97%)
  local copies, waits for them, and re-layouts  2.06 us (3%)
    pallas_call x1, Pallas kernels, on_device(): pl.pallas_call(whole_kernel, name='forces', out_shape=jax.ShapeDtypeStruc...  77.3 us
    unnamed x1, local copies, waits for them, and re-layouts  2.06 us

profile of v3, /device:TPU:1, one launch (start us, length us, event | category | flops | bytes accessed | tf_op | source)
XLA Modules:
  0.0 79.3 jit_solution(3571522730300919775)
XLA Ops:
  0.0 77.3 %forces.1 = f32[512,384]{1,0:T(8,128)} custom-call(s32[4,128]{1,0:T(4,128)} %bitcast.5, s32[2,256]{1,0:T(2,128)} %bitcast.7, s32[4,128]{1,0:T(4,128)} %bitcast.6, s32[2,256]{1,0:T(2,128)} %bitcast.8, s32[1,512]{1,0:T(1,128)} %bitcast.9, f32[512,384]{1,0:T(8,128)} %pos_hbm.1, f32[512,768]{1,0:T(8,128)} %vec_hbm.1), custom_call_target="tpu_custom_call" | custom-call | tf_op jit(solution)/shard_map/forces/pallas_call | solution.py:543
  77.3 2.1 %copy.7 = f32[512,384]{1,0:T(8,128)} copy(f32[512,384]{1,0:T(8,128)} %forces.1) | data formatting | bytes 1572864

commit v4 on v3

--- a/solution.py
+++ b/solution.py
@@ -14,14 +14,14 @@
 WIDTH = 128
 MIDDLE = 2.0
 ROWS = 16
-UNROLL = 2
-CUBE_UNROLL = 4
+UNROLL = 6
+CUBE_UNROLL = 8
 CAP = 4
 BACK = 12
-FAR_GROUPS = 2
+FAR_GROUPS = 4
+SIDE_X = 4
 LOADS = 8
-SIDE_X = 4
-VMEM_LIMIT = 60 * 2**20
+VMEM_LIMIT = 54 * 2**20
 
 
 def high_low(value):
@@ -43,22 +43,6 @@
     upper = square.astype(BF16).astype(F32)
     one = jnp.ones_like(square)
     return couplings(tensor) + list(place) + [upper, square - upper, one, one]
-
-
-def other(step):
-    gx, yz = lax.axis_index("gx"), lax.axis_index("yz")
-    size_yz = lax.axis_size("yz")
-    chips = lax.axis_size("gx") * size_yz // 2
-    side_x, side_z = SIDE_X, size_yz // 2
-    side_y = lax.axis_size("gx") // side_x
-    chip, core = lax.rem(step, chips), step // chips
-    first = lax.rem(chip, side_y)
-    second = first + lax.rem(chip // side_y, side_x)
-    third = second + chip // (side_y * side_x)
-    y = lax.rem(gx // side_x + first, side_y)
-    x = lax.rem(lax.rem(gx, side_x) + second, side_x)
-    z = lax.rem(yz // 2 + third, side_z)
-    return y * side_x + x, z * 2 + lax.rem(lax.rem(yz, 2) + core, 2)
 
 
 def pack_group(step, pos_ref, vec_ref, base_ref, table, packed):
@@ -141,14 +125,17 @@
 
 
 def whole_kernel(
+    ids_hbm,
+    pairs_hbm,
+    coarse_hbm,
+    pos_hbm,
+    vec_hbm,
+    o_ref,
     ids_ref,
     pairs_ref,
     id_rows,
     pair_rows,
     coarse_ref,
-    pos_hbm,
-    vec_hbm,
-    o_ref,
     pos_ref,
     vec_ref,
     packed,
@@ -170,6 +157,7 @@
     send_sem,
     recv_sem,
     bulk_sem,
+    small_sem,
     round_sem,
     *buffers,
 ):
@@ -202,9 +190,23 @@
     for turn, size in ((along_yz, size_yz), (along_gx, size_gx)):
         for step in range(1, size):
             pl.semaphore_signal(barrier, inc=1, device_id=turn(step), device_id_type=MESH)
+    small = [
+        pltpu.make_async_copy(source, target, small_sem.at[k])
+        for k, (source, target) in enumerate(
+            (
+                (ids_hbm, ids_ref),
+                (coarse_hbm, coarse_ref),
+                (pairs_hbm, pairs_ref),
+                (ids_hbm, id_rows),
+                (pairs_hbm, pair_rows),
+            )
+        )
+    ]
     for step in range(LOADS):
         for copy in loads(step):
             copy.start()
+    for copy in small:
+        copy.start()
 
     def pack(step, carry):
         for copy in loads(step):
@@ -220,6 +222,8 @@
     pl.semaphore_wait(barrier, size_yz + size_gx - 2)
     for step in range(1, size_yz):
         pl.semaphore_signal(round_sem, inc=1, device_id=along_yz(step), device_id_type=MESH)
+    for copy in small:
+        copy.wait()
 
     def exchange(source, held, turn, size, sem):
         return [
@@ -242,13 +246,6 @@
             result = result + held[step]
         return result
 
-    mine[...] = cell_sums(coarse_ref, table)
-    over_yz = exchange(mine, near, along_yz, size_yz, 0)
-    over_gx = exchange(total, far, along_gx, size_gx, size_yz)
-    for copy in over_yz:
-        copy.start()
-    pl.semaphore_wait(round_sem, size_yz - 1)
-
     chunk = CAP * 8
     half = chunk // 2
 
@@ -259,8 +256,8 @@
                 source
             ]
 
-    def bulk(step, source, target, pitch, at, size, sem):
-        to_gx, to_yz = other(step)
+    def bulk(to, source, target, pitch, at, size, sem):
+        to_gx, to_yz = to
         device = to_gx * size_yz + to_yz
         return pltpu.make_async_remote_copy(
             src_ref=source.at[pl.ds(pl.multiple_of(device * pitch + at, 8), size)],
@@ -278,45 +275,86 @@
             dst_ref=target.at[rows],
             send_sem=bulk_sem.at[sem],
             recv_sem=bulk_sem.at[sem + 1],
-            device_id=other(1),
+            device_id=along_yz(1),
             device_id_type=MESH,
         )
 
-    def send_first(step, carry):
-        to_gx, to_yz = other(step)
-        pick(to_gx * size_yz + to_yz)
-        bulk(step, send_ref, got_ref, chunk, 0, half, 0).start()
-        return carry
-
-    def send_second(step, carry):
-        bulk(step, send_ref, got_ref, chunk, half, half, 2).start()
-        return carry
-
-    lax.fori_loop(1, 1 + devices // 4, send_first, 0)
+    def to_axes(send):
+        def one(turn):
+            def step(number, carry):
+                send(turn(number))
+                return carry
+
+            return step
+
+        lax.fori_loop(1, size_yz, one(along_yz), 0)
+        lax.fori_loop(1, size_gx, one(along_gx), 0)
+
+    def aside(send, step):
+        for part in range(size_yz - 1):
+            turned = lax.rem(step + part, size_yz - 1)
+            send((lax.rem(gx + step, size_gx), lax.rem(yz + 1 + turned, size_yz)))
+
+    def to_rest(send):
+        def one(step, carry):
+            aside(send, step)
+            return carry
+
+        lax.fori_loop(1, size_gx, one, 0)
+
+    side_x, side_z = SIDE_X, size_yz // 2
+    side_y = size_gx // side_x
+    here = (gx // side_x, lax.rem(gx, side_x), yz // 2, lax.rem(yz, 2))
+
+    def to_chips(send):
+        def turn(second, third, core, first):
+            for ahead in range(first, side_y):
+                y = lax.rem(here[0] + ahead, side_y)
+                x = lax.rem(here[1] + ahead + second, side_x)
+                z = lax.rem(here[2] + ahead + second + third, side_z)
+                send((y * side_x + x, z * 2 + lax.rem(here[3] + core, 2)))
+
+        def one(step, carry):
+            turn(
+                lax.rem(step, side_x),
+                lax.rem(step // side_x, side_z),
+                step // (side_x * side_z),
+                0,
+            )
+            return carry
+
+        turn(0, 0, 0, 1)
+        lax.fori_loop(1, 2 * side_x * side_z, one, 0)
+
+    def send_first(to):
+        pick(to[0] * size_yz + to[1])
+        bulk(to, send_ref, got_ref, chunk, 0, half, 0).start()
+
+    def send_second(to):
+        bulk(to, send_ref, got_ref, chunk, half, half, 2).start()
+
+    def send_back(to):
+        bulk(to, out_ref, back_ref, ROWS, 0, BACK, 4).start()
+
+    to_axes(send_first)
+    mine[...] = cell_sums(coarse_ref, table)
+    over_yz = exchange(mine, near, along_yz, size_yz, 0)
+    over_gx = exchange(total, far, along_gx, size_gx, size_yz)
+    for copy in over_yz:
+        copy.start()
+    pl.semaphore_wait(round_sem, size_yz - 1)
+    to_rest(send_first)
+    to_axes(send_second)
+    to_rest(send_second)
     total[...] = gathered(mine, near, over_yz)
     for copy in over_gx:
         copy.start()
-    lax.fori_loop(1 + devices // 4, devices, send_first, 0)
-    lax.fori_loop(1, devices, send_second, 0)
     pick(me)
     rows = pl.ds(pl.multiple_of(me * chunk, chunk), chunk)
     got_ref[rows, :] = send_ref[rows, :]
     for matrix in matrices:
         matrix[...] = jnp.zeros_like(matrix)
     form_base[...] = jnp.zeros_like(form_base)
-
-    sums = gathered(total, far, over_gx)
-    left = far_left(
-        jnp.concatenate([sums[:, :KC], sums[:, KC:]], axis=0),
-        1.0 / (math.sqrt(blocks * devices * WIDTH / KC) * math.sqrt(KC)),
-    )
-
-    def far_step(step, carry):
-        for part in range(FAR_GROUPS):
-            far_group(step * FAR_GROUPS + part, left, pos_ref, base_ref, o_ref, tiles[part])
-        return carry
-
-    lax.fori_loop(0, blocks // (8 * FAR_GROUPS), far_step, 0)
 
     def came(step, slot, first, last):
         return [
@@ -450,11 +488,19 @@
                 :, k * WIDTH : (k + 1) * WIDTH
             ]
 
-    def send_back(step, carry):
-        bulk(step, out_ref, back_ref, ROWS, 0, BACK, 4).start()
+    to_chips(send_back)
+    sums = gathered(total, far, over_gx)
+    left = far_left(
+        jnp.concatenate([sums[:, :KC], sums[:, KC:]], axis=0),
+        1.0 / (math.sqrt(blocks * devices * WIDTH / KC) * math.sqrt(KC)),
+    )
+
+    def far_step(step, carry):
+        for part in range(FAR_GROUPS):
+            far_group(step * FAR_GROUPS + part, left, pos_ref, base_ref, o_ref, tiles[part])
         return carry
 
-    lax.fori_loop(1, devices, send_back, 0)
+    lax.fori_loop(0, blocks // (8 * FAR_GROUPS), far_step, 0)
     rows = pl.ds(pl.multiple_of(me * ROWS, ROWS), ROWS)
     back_ref[rows, :] = out_ref[rows, :]
     all_of(send_ref, got_ref, half, 0).wait_send()
@@ -526,8 +572,6 @@
 
 
 VM = pl.BlockSpec(memory_space=pltpu.VMEM)
-SM = pl.BlockSpec(memory_space=pltpu.SMEM)
-ANY = pl.BlockSpec(memory_space=pl.ANY)
 
 
 def on_device(positions, vectors, send_slots, pairs, coarse):
@@ -544,9 +588,14 @@
         whole_kernel,
         name="forces",
         out_shape=jax.ShapeDtypeStruct((blocks, 3 * WIDTH), F32),
-        in_specs=[SM, SM, VM, VM, VM, ANY, ANY],
+        in_specs=[pl.BlockSpec(memory_space=pltpu.HBM)] * 5,
         out_specs=VM,
         scratch_shapes=[
+            pltpu.SMEM((CAP, devices), jnp.int32),
+            pltpu.SMEM((2, count), jnp.int32),
+            pltpu.VMEM((CAP, devices), jnp.int32),
+            pltpu.VMEM((2, count), jnp.int32),
+            pltpu.VMEM((1, blocks), jnp.int32),
             rows(blocks, 3 * WIDTH),
             rows(blocks, 6 * WIDTH),
             pltpu.VMEM((blocks, 8, WIDTH), F32),
@@ -568,6 +617,7 @@
             dma((size_yz + size_gx,)),
             dma((size_yz + size_gx,)),
             dma((6,)),
+            dma((5,)),
             pltpu.SemaphoreType.REGULAR,
         ]
         + [rows(192)] * FAR_GROUPS
@@ -575,7 +625,7 @@
         compiler_params=pltpu.CompilerParams(
             vmem_limit_bytes=VMEM_LIMIT, collective_id=0, has_side_effects=True
         ),
-    )(ids, pair_ids, ids, pair_ids, coarse.reshape(1, blocks), positions, vectors)
+    )(ids, pair_ids, coarse.reshape(1, blocks), positions, vectors)
 
 
 def solution(mesh):

time: 79.5 us -> 69.5 us (0.87)
  Pallas kernels: 77.3 us -> 67.3 us
    pallas_call x1, Pallas kernels: 77.3 us -> 67.3 us  [on_device(): pl.pallas_call(whole_kernel, name='forces', out_shape=jax.ShapeDtypeStruc...]
where the time goes in v4:
time: 69.5 us; the launch traced here: 69.3 us
  Pallas kernels  67.3 us (97%)
  local copies, waits for them, and re-layouts  2.06 us (3%)
    pallas_call x1, Pallas kernels, on_device(): pl.pallas_call(whole_kernel, name='forces', out_shape=jax.ShapeDtypeStruc...  67.3 us
    unnamed x1, local copies, waits for them, and re-layouts  2.06 us

profile of v4, /device:TPU:1, one launch (start us, length us, event | category | flops | bytes accessed | tf_op | source)
XLA Modules:
  0.0 69.3 jit_solution(6408885501590506244)
XLA Ops:
  0.0 67.3 %forces.1 = f32[512,384]{1,0:T(8,128)} custom-call(s32[4,128]{1,0:T(4,128)} %bitcast.5, s32[2,256]{1,0:T(2,128)} %bitcast.6, s32[1,512]{1,0:T(1,128)} %bitcast.7, f32[512,384]{1,0:T(8,128)} %pos_hbm.1, f32[512,768]{1,0:T(8,128)} %vec_hbm.1), custom_call_target="tpu_custom_call" | custom-call | tf_op jit(solution)/shard_map/forces/pallas_call | solution.py:587
  67.3 2.1 %copy.7 = f32[512,384]{1,0:T(8,128)} copy(f32[512,384]{1,0:T(8,128)} %forces.1) | data formatting | bytes 1572864

commit v5 on v4

--- a/solution.py
+++ b/solution.py
@@ -14,7 +14,7 @@
 WIDTH = 128
 MIDDLE = 2.0
 ROWS = 16
-UNROLL = 6
+UNROLL = 8
 CUBE_UNROLL = 8
 CAP = 4
 BACK = 12
@@ -352,8 +352,6 @@
     pick(me)
     rows = pl.ds(pl.multiple_of(me * chunk, chunk), chunk)
     got_ref[rows, :] = send_ref[rows, :]
-    for matrix in matrices:
-        matrix[...] = jnp.zeros_like(matrix)
     form_base[...] = jnp.zeros_like(form_base)
 
     def came(step, slot, first, last):
@@ -372,14 +370,17 @@
             one = jnp.ones_like(square)
             values = place + [upper, square - upper, one, one, jnp.zeros_like(square)]
             for row, value in enumerate(values):
-                place_rows_ref[pl.ds(step * 64 * CAP + slot * 8 + row, 8, stride=8 * CAP), :] = value
+                place_rows_ref[
+                    pl.ds((slot * devices + step * 8) * 8 + row, 8, stride=8), :
+                ] = value
         return carry
 
     lax.fori_loop(0, devices // 8, place_rows, 0)
     row = lax.broadcasted_iota(jnp.int32, (8, WIDTH), 0)
 
     def tile_of(base, side, number):
-        return base[jnp.maximum(pairs_ref[side, number], 0)]
+        slot = jnp.maximum(pairs_ref[side, number], 0)
+        return base[lax.rem(slot, CAP) * devices + lax.div(slot, CAP)]
 
     def cube_step(step, carry):
         for part in range(CUBE_UNROLL):
@@ -411,7 +412,7 @@
             line = [2.0 * got[3] * inverse, 2.0 * got[4] * inverse, (1.0 - square) * inverse]
             for row, value in enumerate(couplings([[b * l for l in line] for b in got[:3]])):
                 form_rows_ref[
-                    pl.ds(step * 8 * ROWS * CAP + slot * ROWS + row, 8, stride=ROWS * CAP), :
+                    pl.ds((slot * devices + step * 8) * ROWS + row, 8, stride=ROWS), :
                 ] = value
         return carry
 
@@ -429,7 +430,7 @@
         matrix[pl.ds(0, WIDTH), :] = high
         matrix[pl.ds(WIDTH, WIDTH), :] = low
 
-    def drain(number, at, matrix):
+    def drain(number, matrix):
         value = matrix[...]
         places = [[tile_of(place_base, side, number + i) for i in range(2)] for side in range(2)]
         first, second = [[stacked(tile) for tile in side] for side in places]
@@ -447,29 +448,35 @@
             on_second = on_b[i * ROWS : (i + 1) * ROWS, i * WIDTH : (i + 1) * WIDTH]
             for side, got in enumerate((on_first, on_second)):
                 force = places[side][i] * got[5:6] - (got[:8] + got[8:])
-                forces[side, pl.ds(pl.multiple_of((at + i) * 8, 8), 8), :] = force
+                forces[side, pl.ds(pl.multiple_of((number + i) * 8, 8), 8), :] = force
 
     even, odd = matrices[:UNROLL], matrices[UNROLL:]
 
-    def half_step(number, filled, drained):
+    size = 2 * UNROLL
+    halves = count // size
+
+    def half_step(filling, filled, draining, drained):
         for part in range(UNROLL):
-            fill(jnp.minimum(number + 2 * part, count - 2), filled[part])
-            at = number + 2 * part
-            before = jnp.clip(at - 2 * UNROLL, 0, count - 2)
-            drain(before, at, drained[part])
+            if filling is not None:
+                fill(filling * size + 2 * part, filled[part])
+            if draining is not None:
+                drain(draining * size + 2 * part, drained[part])
 
     def pair_step(step, carry):
-        half_step(step * 4 * UNROLL, even, odd)
-        half_step(step * 4 * UNROLL + 2 * UNROLL, odd, even)
+        half_step(2 * step + 1, odd, 2 * step, even)
+        half_step(2 * step + 2, even, 2 * step + 1, odd)
         return carry
 
-    lax.fori_loop(0, pl.cdiv(count + 2 * UNROLL, 4 * UNROLL), pair_step, 0)
+    half_step(0, even, None, None)
+    lax.fori_loop(0, halves // 2 - 1, pair_step, 0)
+    half_step(halves - 1, odd, halves - 2, even)
+    half_step(None, None, halves - 1, odd)
     parts = []
     for side in range(2):
         parts.append(
             jnp.concatenate(
                 [
-                    forces[side, pl.ds(16 * UNROLL + k, count, stride=8), :]
+                    forces[side, pl.ds(k, count, stride=8), :]
                     for k in range(3)
                 ],
                 axis=1,
@@ -606,7 +613,7 @@
             pltpu.VMEM((slots, 8, WIDTH), F32),
             pltpu.VMEM((slots, ROWS, WIDTH), F32),
             rows(count * WIDTH // 2, 2 * WIDTH),
-            pltpu.VMEM((2, (count + 6 * UNROLL) * 8, WIDTH), F32),
+            pltpu.VMEM((2, count * 8, WIDTH), F32),
             rows(devices * ROWS),
             rows(devices * ROWS),
             rows(8),

time: 69.5 us -> 67.6 us (0.973)
  Pallas kernels: 67.3 us -> 65.3 us
    pallas_call x1, Pallas kernels: 67.3 us -> 65.3 us  [on_device(): pl.pallas_call(whole_kernel, name='forces', out_shape=jax.ShapeDtypeStruc...]
where the time goes in v5:
time: 67.6 us; the launch traced here: 67.4 us
  Pallas kernels  65.3 us (97%)
  local copies, waits for them, and re-layouts  2.06 us (3%)
    pallas_call x1, Pallas kernels, on_device(): pl.pallas_call(whole_kernel, name='forces', out_shape=jax.ShapeDtypeStruc...  65.3 us
    unnamed x1, local copies, waits for them, and re-layouts  2.06 us

profile of v5, /device:TPU:1, one launch (start us, length us, event | category | flops | bytes accessed | tf_op | source)
XLA Modules:
  0.0 67.4 jit_solution(11726180793184271928)
XLA Ops:
  0.0 65.3 %forces.1 = f32[512,384]{1,0:T(8,128)} custom-call(s32[4,128]{1,0:T(4,128)} %bitcast.5, s32[2,256]{1,0:T(2,128)} %bitcast.6, s32[1,512]{1,0:T(1,128)} %bitcast.7, f32[512,384]{1,0:T(8,128)} %pos_hbm.1, f32[512,768]{1,0:T(8,128)} %vec_hbm.1), custom_call_target="tpu_custom_call" | custom-call | tf_op jit(solution)/shard_map/forces/pallas_call | solution.py:594
  65.3 2.1 %copy.7 = f32[512,384]{1,0:T(8,128)} copy(f32[512,384]{1,0:T(8,128)} %forces.1) | data formatting | bytes 1572864

commit v6 on v5

--- a/solution.py
+++ b/solution.py
@@ -344,8 +344,7 @@
         copy.start()
     pl.semaphore_wait(round_sem, size_yz - 1)
     to_rest(send_first)
-    to_axes(send_second)
-    to_rest(send_second)
+    to_chips(send_second)
     total[...] = gathered(mine, near, over_yz)
     for copy in over_gx:
         copy.start()

time: 67.6 us -> 66.3 us (0.981)
  Pallas kernels: 65.3 us -> 64 us
    pallas_call x1, Pallas kernels: 65.3 us -> 64 us  [on_device(): pl.pallas_call(whole_kernel, name='forces', out_shape=jax.ShapeDtypeStruc...]
where the time goes in v6:
time: 66.3 us; the launch traced here: 66.1 us
  Pallas kernels  64 us (97%)
  local copies, waits for them, and re-layouts  2.06 us (3%)
    pallas_call x1, Pallas kernels, on_device(): pl.pallas_call(whole_kernel, name='forces', out_shape=jax.ShapeDtypeStruc...  64 us
    unnamed x1, local copies, waits for them, and re-layouts  2.06 us

profile of v6, /device:TPU:1, one launch (start us, length us, event | category | flops | bytes accessed | tf_op | source)
XLA Modules:
  0.0 66.1 jit_solution(4203213683465315252)
XLA Ops:
  0.0 64.0 %forces.1 = f32[512,384]{1,0:T(8,128)} custom-call(s32[4,128]{1,0:T(4,128)} %bitcast.5, s32[2,256]{1,0:T(2,128)} %bitcast.6, s32[1,512]{1,0:T(1,128)} %bitcast.7, f32[512,384]{1,0:T(8,128)} %pos_hbm.1, f32[512,768]{1,0:T(8,128)} %vec_hbm.1), custom_call_target="tpu_custom_call" | custom-call | tf_op jit(solution)/shard_map/forces/pallas_call | solution.py:593
  64.1 2.1 %copy.7 = f32[512,384]{1,0:T(8,128)} copy(f32[512,384]{1,0:T(8,128)} %forces.1) | data formatting | bytes 1572864
